TPU v7x, 128 devices: a whole 4x4x4 slice. The times are simulated.
128 devices in a mesh: pu: 8 (over y, core), pv: 16 (over z, x).
Axes of the slice: x: 4, y: 4, z: 4, core: 2. Of those that a mesh axis runs over, the one named last changes fastest.
Arguments:
- density: bfloat16 [48, 96, 128, 768], P('pu', 'pv'), may hold values from -6 to 6
- near_blocks: bfloat16 [48, 96, 6, 128, 128], P('pu', 'pv'), may hold values from -0.21875 to 0.21875
- neighbours: int32 [48, 96, 6], P('pu', 'pv'), may hold values from 0 to 9
- far_right: bfloat16 [48, 96, 128, 128], P('pu', 'pv'), may hold values from -0.09375 to 0.09375
- far_left: float32 [8, 16, 1024, 128], P('pu', 'pv'), may hold values from -0.1875 to 0.1875
- sketch: float32 [256, 128], replicated, may hold values from -0.375 to 0.375
- patch_order: int32 [128], replicated, may hold values from 0 to 127, each once
Outputs:
- corrected: bfloat16 [48, 96, 128, 768], P('pu', 'pv')
- far_field: float32 [1024, 768], P('pu', 'pv')
Inputs may be any that keep to these rules, and one draw needn't show every extreme that they name: `neighbours`: entry e < 9 names the block displaced by e // 3 - 1 patch rows and e % 3 - 1 patch columns (e = 4 is the block itself); 9 marks an empty slot. `patch_order`: A permutation of the patches.
All inputs are finite; a program needn't handle non-finite values.
Results may differ from a plain program's by a relative error of at most 0.0028.
Values may be sent and summed in bfloat16 or wider, within the bound.
A program may use at most 256 MiB of HBM per device.

v0:
```python
import jax
import jax.numpy as jnp
from jax import lax
from jax.sharding import PartitionSpec as P

highest = lax.Precision.HIGHEST
empty_slot = 9


def extended_2(block, sides, width):
    for axis, dim in sides:
        count = lax.axis_size(axis)
        forward = [(i, i + 1) for i in range(count - 1)]
        backward = [(target, source) for source, target in forward]
        low = lax.ppermute(
            lax.slice_in_dim(block, block.shape[dim] - width, None, axis=dim), axis, forward
        )
        high = lax.ppermute(lax.slice_in_dim(block, 0, width, axis=dim), axis, backward)
        block = jnp.concatenate([low, block, high], axis=dim)
    return block


def from_partner(value, axis, distance):
    mask = 2**distance
    pairs = [(source, source ^ mask) for source in range(lax.axis_size(axis))]
    return lax.ppermute(value, axis, pairs)


def merge_pair(first_left, first_coef, second_left, second_coef, sketch):
    stacked = jnp.concatenate([first_left, second_left], axis=1)
    coeff_pairs = jnp.concatenate([first_coef, second_coef], axis=0)
    gram_matrix = jnp.dot(stacked.T, stacked, precision=highest)
    reduced = jnp.dot(sketch.T, gram_matrix, precision=highest)
    inner_gram = jnp.dot(reduced, sketch, precision=highest)
    inner_gram = 0.5 * (inner_gram + inner_gram.T)
    factor = jnp.linalg.cholesky(inner_gram)
    sketched = jnp.dot(stacked, sketch, precision=highest)
    new_left = lax.linalg.triangular_solve(factor, sketched.T, left_side=True, lower=True).T
    new_coef = lax.linalg.triangular_solve(
        factor, jnp.dot(reduced, coeff_pairs, precision=highest), left_side=True, lower=True
    )
    return (new_left, new_coef)


def mine_leads(group_keys, position, tree_level):
    block_min = group_keys.reshape(-1, 1 << tree_level).min(axis=1)
    mine_key = block_min[position >> tree_level]
    their_key = block_min[position >> tree_level ^ 1]
    return mine_key < their_key


def ordered_merge(
    mine_left, mine_coef, other_left, other_coef, group_keys, position, tree_level, sketch
):
    mine_first = mine_leads(group_keys, position, tree_level)
    first_left = jnp.where(mine_first, mine_left, other_left)
    second_left = jnp.where(mine_first, other_left, mine_left)
    first_coef = jnp.where(mine_first, mine_coef, other_coef)
    second_coef = jnp.where(mine_first, other_coef, mine_coef)
    return merge_pair(first_left, first_coef, second_left, second_coef, sketch)


def near_field(density, extended, near_blocks, neighbours):
    block_rows = density.shape[0]
    block_cols = density.shape[1]
    row_base = jnp.arange(block_rows, dtype=jnp.int32)[:, None]
    col_base = jnp.arange(block_cols, dtype=jnp.int32)[None, :]
    summed = jnp.zeros(density.shape, jnp.float32)
    for position in range(neighbours.shape[2]):
        slot_links = neighbours[:, :, position]
        stencil = jnp.minimum(slot_links, 8)
        near_rows = extended[row_base + stencil // 3, col_base + stencil % 3]
        product = jnp.einsum(
            "ijab,ijbr->ijar",
            near_blocks[:, :, position],
            near_rows,
            preferred_element_type=jnp.float32,
        )
        summed = summed + jnp.where((slot_links < empty_slot)[:, :, None, None], product, 0.0)
    return (density.astype(jnp.float32) + summed).astype(jnp.bfloat16)


def corrected_density(density, near_blocks, neighbours):
    extended = extended_2(density, (("pu", 0), ("pv", 1)), 1)
    return near_field(density, extended, near_blocks, neighbours)


def per_device(density, near_blocks, neighbours, far_right, far_left, sketch, patch_order):
    pu_count = lax.axis_size("pu")
    pv_count = lax.axis_size("pv")
    pu_index = lax.axis_index("pu")
    pv_index = lax.axis_index("pv")
    key_grid = patch_order.reshape(pu_count, pv_count)
    row_keys = lax.dynamic_index_in_dim(key_grid, pu_index, 0, keepdims=False)
    column_keys = key_grid.min(axis=1)
    left_now = far_left[0, 0]
    corrected = corrected_density(density, near_blocks, neighbours)
    coef_now = jnp.einsum("ijar,ijak->rk", far_right, corrected, preferred_element_type=jnp.float32)
    for tree_level in range(pv_count.bit_length() - 1):
        other_left, other_coef = from_partner((left_now, coef_now), "pv", tree_level)
        left_now, coef_now = ordered_merge(
            left_now, coef_now, other_left, other_coef, row_keys, pv_index, tree_level, sketch
        )
    for tree_level in range(pu_count.bit_length() - 1):
        other_left, other_coef = from_partner((left_now, coef_now), "pu", tree_level)
        left_now, coef_now = ordered_merge(
            left_now, coef_now, other_left, other_coef, column_keys, pu_index, tree_level, sketch
        )
    obs_rows = left_now.shape[0] // pu_count
    rhs_cols = coef_now.shape[1] // pv_count
    left_rows = lax.dynamic_slice_in_dim(left_now, pu_index * obs_rows, obs_rows, 0)
    coef_cols = lax.dynamic_slice_in_dim(coef_now, pv_index * rhs_cols, rhs_cols, 1)
    far_field = jnp.dot(left_rows, coef_cols, precision=highest)
    return (corrected, far_field)


def solution(mesh):
    in_specs = (
        P("pu", "pv", None, None),
        P("pu", "pv", None, None, None),
        P("pu", "pv", None),
        P("pu", "pv", None, None),
        P("pu", "pv", None, None),
        P(),
        P(),
    )
    out_specs = (P("pu", "pv", None, None), P("pu", "pv"))
    return jax.shard_map(
        per_device, mesh=mesh, in_specs=in_specs, out_specs=out_specs, check_vma=False
    )
```

profile of v0, /device:TPU:1, one launch (start us, length us, event | category | flops | bytes accessed | tf_op | source)
XLA Modules:
  0.0 528.7 jit_solution(8989616937113093669)
XLA Ops:
  21.2 11.7 %cholesky.119 = f32[128,128]{1,0:T(8,128)S(1)} custom-call(f32[128,128]{1,0:T(8,128)S(1)} %fusion.94), custom_call_target="Cholesky" | custom-call | tf_op jit(solution)/shard_map/jit(cholesky)/cholesky | solution.py:36
  34.3 9.8 %custom-call.32 = f32[1,128,128]{1,2,0:T(8,128)S(1)} custom-call(f32[1,128,128]{2,1,0:T(8,128)S(1)} %fusion.53), custom_call_target="InvertDiagBlocksLowerTriangular" | custom-call | tf_op jit(solution)/shard_map/triangular_solve/custom-call.0 | solution.py:38
  50.2 10.0 %collective-permute-done.5 = f32[1024,128]{0,1:T(8,128)S(1)} collective-permute-done((f32[1024,128]{0,1:T(8,128)S(1)}, f32[1024,128]{0,1:T(8,128)S(1)}, u32[]{:S(2)}, u32[]{:S(2)}) %collective-permute-start.5) | collective-permute-done | bytes 524320 | tf_op jit(solution)/shard_map/ppermute | solution.py:26
  64.4 11.7 %cholesky.130 = f32[128,128]{1,0:T(8,128)S(1)} custom-call(f32[128,128]{1,0:T(8,128)S(1)} %fusion.89), custom_call_target="Cholesky" | custom-call | tf_op jit(solution)/shard_map/jit(cholesky)/cholesky | solution.py:36
  77.4 9.8 %custom-call.33 = f32[1,128,128]{1,2,0:T(8,128)S(1)} custom-call(f32[1,128,128]{2,1,0:T(8,128)S(1)} %fusion.54), custom_call_target="InvertDiagBlocksLowerTriangular" | custom-call | tf_op jit(solution)/shard_map/triangular_solve/custom-call.0 | solution.py:38
  90.1 10.3 %copy.45 = bf16[6,6,128,768]{2,3,1,0:T(8,128)(2,1)} copy(bf16[6,6,128,768]{3,2,1,0:T(8,128)(2,1)} %param.12) | data formatting | bytes 14155776 | tf_op args[0]
  114.8 11.7 %cholesky.141 = f32[128,128]{1,0:T(8,128)S(1)} custom-call(f32[128,128]{1,0:T(8,128)S(1)} %fusion.84), custom_call_target="Cholesky" | custom-call | tf_op jit(solution)/shard_map/jit(cholesky)/cholesky | solution.py:36
  127.9 9.8 %custom-call.34 = f32[1,128,128]{1,2,0:T(8,128)S(1)} custom-call(f32[1,128,128]{2,1,0:T(8,128)S(1)} %fusion.55), custom_call_target="InvertDiagBlocksLowerTriangular" | custom-call | tf_op jit(solution)/shard_map/triangular_solve/custom-call.0 | solution.py:38
  146.3 8.7 %collective-permute-done.7 = f32[1024,128]{0,1:T(8,128)S(1)} collective-permute-done((f32[1024,128]{0,1:T(8,128)S(1)}, f32[1024,128]{0,1:T(8,128)S(1)}, u32[]{:S(2)}, u32[]{:S(2)}) %collective-permute-start.7) | collective-permute-done | bytes 524320 | tf_op jit(solution)/shard_map/ppermute | solution.py:26
  157.5 11.7 %cholesky.152 = f32[128,128]{1,0:T(8,128)S(1)} custom-call(f32[128,128]{1,0:T(8,128)S(1)} %fusion.79), custom_call_target="Cholesky" | custom-call | tf_op jit(solution)/shard_map/jit(cholesky)/cholesky | solution.py:36
  170.5 9.8 %custom-call.35 = f32[1,128,128]{1,2,0:T(8,128)S(1)} custom-call(f32[1,128,128]{2,1,0:T(8,128)S(1)} %fusion.56), custom_call_target="InvertDiagBlocksLowerTriangular" | custom-call | tf_op jit(solution)/shard_map/triangular_solve/custom-call.0 | solution.py:38
  203.9 11.7 %cholesky.163 = f32[128,128]{1,0:T(8,128)S(1)} custom-call(f32[128,128]{1,0:T(8,128)S(1)} %fusion.74), custom_call_target="Cholesky" | custom-call | tf_op jit(solution)/shard_map/jit(cholesky)/cholesky | solution.py:36
  216.9 9.8 %custom-call.36 = f32[1,128,128]{1,2,0:T(8,128)S(1)} custom-call(f32[1,128,128]{2,1,0:T(8,128)S(1)} %fusion.57), custom_call_target="InvertDiagBlocksLowerTriangular" | custom-call | tf_op jit(solution)/shard_map/triangular_solve/custom-call.0 | solution.py:38
  238.2 10.8 %pad_maximum_fusion = bf16[8,8,128,768]{3,2,1,0:T(8,128)(2,1)} fusion(bf16[8,1,128,768]{3,2,1,0:T(8,128)(2,1)} %collective-permute-done.3, bf16[8,6,128,768]{3,2,1,0:T(8,128)(2,1)} %constant_dynamic-update-slice_fusion, bf16[8,1,128,768]{3,2,1,0:T(8,128)(2,1)} %collective-permute-done.2), kind=kLoop, calls=%fused_computation.8 | loop fusion | flops 12582912 | bytes 25165824 | tf_op jit(solution)/shard_map/concatenate | solution.py:19
  248.9 10.9 %gather_fusion = bf16[36,128,768]{2,1,0:T(8,128)(2,1)} fusion(bf16[8,8,128,768]{3,2,1,0:T(8,128)(2,1)} %pad_maximum_fusion, s32[36]{0:T(128)S(1)} %reshape.182), kind=kCustom, calls=%fused_computation | custom fusion | bytes 14156064 | tf_op jit(solution)/shard_map/gather | solution.py:72
  259.8 11.0 %gather_fusion.4 = bf16[36,128,768]{2,1,0:T(8,128)(2,1)} fusion(bf16[8,8,128,768]{3,2,1,0:T(8,128)(2,1)} %pad_maximum_fusion, s32[36]{0:T(128)S(1)} %reshape.206), kind=kCustom, calls=%fused_computation.4 | custom fusion | bytes 14156064 | tf_op jit(solution)/shard_map/gather | solution.py:72
  270.8 10.6 %fusion.10 = f32[6,6,768,128]{3,2,1,0:T(8,128)} fusion(bf16[6,6,128,768]{3,2,1,0:T(8,128)(2,1)} %bitcast.291, bf16[6,6,6,128,128]{4,3,2,1,0:T(8,128)(2,1)} %param.13), kind=kOutput, calls=%fused_computation.32 | convolution fusion | flops 905969664 | bytes 22413312 | tf_op jit(solution)/shard_map/ijab,ijbr->ijar/dot_general | solution.py:73
  281.4 7.4 %fusion.2 = f32[6,6,768,128]{3,2,1,0:T(8,128)} fusion(bf16[6,6,128,768]{3,2,1,0:T(8,128)(2,1)S(1)} %bitcast.292, bf16[6,6,6,128,128]{4,3,2,1,0:T(8,128)(2,1)} %param.13), kind=kOutput, calls=%fused_computation.24 | convolution fusion | flops 905969664 | bytes 22413312 | tf_op jit(solution)/shard_map/ijab,ijbr->ijar/dot_general | solution.py:73
  288.8 11.0 %gather_fusion.3 = bf16[36,128,768]{2,1,0:T(8,128)(2,1)} fusion(bf16[8,8,128,768]{3,2,1,0:T(8,128)(2,1)} %pad_maximum_fusion, s32[36]{0:T(128)S(1)} %reshape.200), kind=kCustom, calls=%fused_computation.3 | custom fusion | bytes 14156064 | tf_op jit(solution)/shard_map/gather | solution.py:72
  299.8 10.3 %fusion.4 = f32[6,6,768,128]{3,2,1,0:T(8,128)} fusion(bf16[6,6,128,768]{3,2,1,0:T(8,128)(2,1)} %bitcast.293, bf16[6,6,6,128,128]{4,3,2,1,0:T(8,128)(2,1)} %param.13), kind=kOutput, calls=%fused_computation.26 | convolution fusion | flops 905969664 | bytes 22413312 | tf_op jit(solution)/shard_map/ijab,ijbr->ijar/dot_general | solution.py:73
  310.1 11.2 %gather_fusion.2 = bf16[36,128,768]{2,1,0:T(8,128)(2,1)} fusion(bf16[8,8,128,768]{3,2,1,0:T(8,128)(2,1)} %pad_maximum_fusion, s32[36]{0:T(128)S(1)} %reshape.194), kind=kCustom, calls=%fused_computation.2 | custom fusion | bytes 14156064 | tf_op jit(solution)/shard_map/gather | solution.py:72
  321.3 10.3 %fusion.6 = f32[6,6,768,128]{3,2,1,0:T(8,128)} fusion(bf16[6,6,128,768]{3,2,1,0:T(8,128)(2,1)} %bitcast.294, bf16[6,6,6,128,128]{4,3,2,1,0:T(8,128)(2,1)} %param.13), kind=kOutput, calls=%fused_computation.28 | convolution fusion | flops 905969664 | bytes 22413312 | tf_op jit(solution)/shard_map/ijab,ijbr->ijar/dot_general | solution.py:73
  331.6 11.0 %gather_fusion.1 = bf16[36,128,768]{2,1,0:T(8,128)(2,1)} fusion(bf16[8,8,128,768]{3,2,1,0:T(8,128)(2,1)} %pad_maximum_fusion, s32[36]{0:T(128)S(1)} %reshape.188), kind=kCustom, calls=%fused_computation.1 | custom fusion | bytes 14156064 | tf_op jit(solution)/shard_map/gather | solution.py:72
  342.6 10.3 %fusion.8 = f32[6,6,768,128]{3,2,1,0:T(8,128)} fusion(bf16[6,6,128,768]{3,2,1,0:T(8,128)(2,1)} %bitcast.295, bf16[6,6,6,128,128]{4,3,2,1,0:T(8,128)(2,1)} %param.13), kind=kOutput, calls=%fused_computation.30 | convolution fusion | flops 905969664 | bytes 22413312 | tf_op jit(solution)/shard_map/ijab,ijbr->ijar/dot_general | solution.py:73
  353.0 11.0 %gather_fusion.5 = bf16[36,128,768]{2,1,0:T(8,128)(2,1)} fusion(bf16[8,8,128,768]{3,2,1,0:T(8,128)(2,1)} %pad_maximum_fusion, s32[36]{0:T(128)S(1)} %reshape.212), kind=kCustom, calls=%fused_computation.5 | custom fusion | bytes 14156064 | tf_op jit(solution)/shard_map/gather | solution.py:72
  364.0 32.2 %fusion = bf16[6,6,128,768]{2,3,1,0:T(8,128)(2,1)} fusion(f32[6,6,768,128]{3,2,1,0:T(8,128)} %fusion.2, f32[6,6,768,128]{3,2,1,0:T(8,128)} %fusion.4, f32[6,6,768,128]{3,2,1,0:T(8,128)} %fusion.6, f32[6,6,768,128]{3,2,1,0:T(8,128)} %fusion.8, f32[6,6,768,128]{3,2,1,0:T(8,128)} %fusion.10, bf16[6,6,128,768]{2,3,1,0:T(8,128)(2,1)} %copy.45, ...), kind=kOutput, calls=%fused_computation.7 | convolution fusion | flops 955514880 | bytes 93192408 | tf_op jit(solution)/shard_map/ijab,ijbr->ijar/dot_general | solution.py:73
  396.2 10.3 %copy.80 = bf16[6,6,128,768]{3,2,1,0:T(8,128)(2,1)} copy(bf16[6,6,128,768]{2,3,1,0:T(8,128)(2,1)} %fusion) | data formatting | bytes 14155776
  417.7 11.7 %cholesky.174 = f32[128,128]{1,0:T(8,128)S(1)} custom-call(f32[128,128]{1,0:T(8,128)S(1)} %fusion.69), custom_call_target="Cholesky" | custom-call | tf_op jit(solution)/shard_map/jit(cholesky)/cholesky | solution.py:36
  430.7 10.4 %custom-call.37 = f32[1,128,128]{1,2,0:T(8,128)} custom-call(f32[1,128,128]{2,1,0:T(8,128)S(1)} %fusion.58), custom_call_target="InvertDiagBlocksLowerTriangular" | custom-call | tf_op jit(solution)/shard_map/triangular_solve/custom-call.0 | solution.py:38
  486.0 11.7 %cholesky.185 = f32[128,128]{1,0:T(8,128)S(1)} custom-call(f32[128,128]{1,0:T(8,128)S(1)} %fusion.64), custom_call_target="Cholesky" | custom-call | tf_op jit(solution)/shard_map/jit(cholesky)/cholesky | solution.py:36
  502.3 9.8 %custom-call.38 = f32[1,128,128]{1,2,0:T(8,128)S(1)} custom-call(f32[1,128,128]{2,1,0:T(8,128)S(1)} %fusion.59), custom_call_target="InvertDiagBlocksLowerTriangular" | custom-call | tf_op jit(solution)/shard_map/triangular_solve/custom-call.0 | solution.py:38
  519.1 7.3 %collective-permute-done.17 = f32[128,768]{1,0:T(8,128)S(1)} collective-permute-done((f32[128,768]{1,0:T(8,128)S(1)}, f32[128,768]{1,0:T(8,128)S(1)}, u32[]{:S(2)}, u32[]{:S(2)}) %collective-permute-start.17) | collective-permute-done | bytes 393248 | tf_op jit(solution)/shard_map/ppermute | solution.py:26
  (236 shorter events, 162.1 us)
Async XLA Ops:
  0.6 405.9 %copy-start = (bf16[6,6,128,128]{3,2,1,0:T(8,128)(2,1)S(1)}, bf16[6,6,128,128]{3,2,1,0:T(8,128)(2,1)}, u32[]{:S(2)}) copy-start(bf16[6,6,128,128]{3,2,1,0:T(8,128)(2,1)} %param.15) | copy-start | bytes 3538948
  0.7 15.4 %collective-permute-start.4 = (f32[1024,128]{1,0:T(8,128)}, f32[1024,128]{1,0:T(8,128)S(1)}, u32[]{:S(2)}, u32[]{:S(2)}) collective-permute-start(f32[1024,128]{1,0:T(8,128)} %bitcast.297), channel_id=1, source_target_pairs={{0,1},{1,0},{2,3},{3,2},{4,5},{5,4},{6,7},{7,6},{8,9},{9,8},{10,11... | collective-permute-start | bytes 1572872 | tf_op jit(solution)/shard_map/ppermute | solution.py:26
  6.0 138.0 %collective-permute-start = (bf16[1,6,128,768]{3,2,1,0:T(8,128)(2,1)}, bf16[1,6,128,768]{3,2,1,0:T(8,128)(2,1)}, u32[]{:S(2)}, u32[]{:S(2)}) collective-permute-start(bf16[1,6,128,768]{3,2,1,0:T(8,128)(2,1)} %get-tuple-element.12), channel_id=1, source_target_pairs={{0,16},{16,32},{32,48},{48,64},{64,80},{80,96},{96,112},{1,17},{17... | collective-permute-start | bytes 3538952 | tf_op jit(solution)/shard_map/ppermute | solution.py:15
  10.0 181.2 %collective-permute-start.1 = (bf16[1,6,128,768]{3,2,1,0:T(8,128)(2,1)}, bf16[1,6,128,768]{3,2,1,0:T(8,128)(2,1)}, u32[]{:S(2)}, u32[]{:S(2)}) collective-permute-start(bf16[1,6,128,768]{3,2,1,0:T(8,128)(2,1)} %get-tuple-element.11), channel_id=1, source_target_pairs={{16,0},{32,16},{48,32},{64,48},{80,64},{96,80},{112,96},{17,1},{33... | collective-permute-start | bytes 3538952 | tf_op jit(solution)/shard_map/ppermute | solution.py:18
  44.1 33.3 %copy-start.13 = (f32[1,128,128]{1,2,0:T(8,128)}, f32[1,128,128]{1,2,0:T(8,128)S(1)}, u32[]{:S(2)}) copy-start(f32[1,128,128]{1,2,0:T(8,128)S(1)} %custom-call.32) | copy-start | bytes 196612
  44.8 15.4 %collective-permute-start.5 = (f32[1024,128]{0,1:T(8,128)S(1)}, f32[1024,128]{0,1:T(8,128)S(1)}, u32[]{:S(2)}, u32[]{:S(2)}) collective-permute-start(f32[1024,128]{0,1:T(8,128)S(1)} %convolution_bitcast_fusion.11), channel_id=1, source_target_pairs={{0,2},{1,3},{2,0},{3,1},{4,6},{5,7},{6,4},{7,5},{8,10},{9,11},{10,... | collective-permute-start | bytes 1572872 | tf_op jit(solution)/shard_map/ppermute | solution.py:26
  87.9 22.7 %collective-permute-start.6 = (f32[1024,128]{0,1:T(8,128)S(1)}, f32[1024,128]{0,1:T(8,128)S(1)}, u32[]{:S(2)}, u32[]{:S(2)}) collective-permute-start(f32[1024,128]{0,1:T(8,128)S(1)} %convolution_bitcast_fusion.9), channel_id=1, source_target_pairs={{0,4},{1,5},{2,6},{3,7},{4,0},{5,1},{6,2},{7,3},{8,12},{9,13},{10,... | collective-permute-start | bytes 1572872 | tf_op jit(solution)/shard_map/ppermute | solution.py:26
  114.2 68.6 %copy-start.3 = (f32[256,128]{1,0:T(8,128)}, f32[256,128]{1,0:T(8,128)S(1)}, u32[]{:S(2)}) copy-start(f32[256,128]{1,0:T(8,128)S(1)} %fusion.197) | copy-start | bytes 393220
  140.2 14.9 %collective-permute-start.7 = (f32[1024,128]{0,1:T(8,128)S(1)}, f32[1024,128]{0,1:T(8,128)S(1)}, u32[]{:S(2)}, u32[]{:S(2)}) collective-permute-start(f32[1024,128]{0,1:T(8,128)S(1)} %convolution_bitcast_fusion.7), channel_id=1, source_target_pairs={{0,8},{1,9},{2,10},{3,11},{4,12},{5,13},{6,14},{7,15},{8,0},{9,1},... | collective-permute-start | bytes 1572872 | tf_op jit(solution)/shard_map/ppermute | solution.py:26
  156.8 34.4 %copy-start.5 = (f32[256,128]{1,0:T(8,128)}, f32[256,128]{1,0:T(8,128)S(1)}, u32[]{:S(2)}) copy-start(f32[256,128]{1,0:T(8,128)S(1)} %fusion.199) | copy-start | bytes 393220
  182.8 18.7 %collective-permute-start.8 = (f32[1024,128]{0,1:T(8,128)S(1)}, f32[1024,128]{0,1:T(8,128)S(1)}, u32[]{:S(2)}, u32[]{:S(2)}) collective-permute-start(f32[1024,128]{0,1:T(8,128)S(1)} %convolution_bitcast_fusion.5), channel_id=1, source_target_pairs={{0,16},{16,0},{32,48},{48,32},{64,80},{80,64},{96,112},{112,96},{1... | collective-permute-start | bytes 1572872 | tf_op jit(solution)/shard_map/ppermute | solution.py:26
  197.6 35.5 %collective-permute-start.2 = (bf16[8,1,128,768]{3,2,1,0:T(8,128)(2,1)}, bf16[8,1,128,768]{3,2,1,0:T(8,128)(2,1)}, u32[]{:S(2)}, u32[]{:S(2)}) collective-permute-start(bf16[8,1,128,768]{3,2,1,0:T(8,128)(2,1)} %get-tuple-element.9), channel_id=1, source_target_pairs={{0,1},{1,2},{2,3},{3,4},{4,5},{5,6},{6,7},{7,8},{8,9},{9,10},{10,1... | collective-permute-start | bytes 4718600 | tf_op jit(solution)/shard_map/ppermute | solution.py:15
  200.0 38.1 %collective-permute-start.3 = (bf16[8,1,128,768]{3,2,1,0:T(8,128)(2,1)}, bf16[8,1,128,768]{3,2,1,0:T(8,128)(2,1)}, u32[]{:S(2)}, u32[]{:S(2)}) collective-permute-start(bf16[8,1,128,768]{3,2,1,0:T(8,128)(2,1)} %get-tuple-element.10), channel_id=1, source_target_pairs={{1,0},{2,1},{3,2},{4,3},{5,4},{6,5},{7,6},{8,7},{9,8},{10,9},{11,1... | collective-permute-start | bytes 4718600 | tf_op jit(solution)/shard_map/ppermute | solution.py:18
  203.2 45.7 %copy-start.7 = (f32[256,128]{1,0:T(8,128)}, f32[256,128]{1,0:T(8,128)S(1)}, u32[]{:S(2)}) copy-start(f32[256,128]{1,0:T(8,128)S(1)} %fusion.201) | copy-start | bytes 393220
  226.8 22.2 %copy-start.18 = (f32[1,128,128]{1,2,0:T(8,128)}, f32[1,128,128]{1,2,0:T(8,128)S(1)}, u32[]{:S(2)}) copy-start(f32[1,128,128]{1,2,0:T(8,128)S(1)} %custom-call.36) | copy-start | bytes 196612
  229.2 184.2 %collective-permute-start.9 = (f32[1024,128]{0,1:T(8,128)S(1)}, f32[1024,128]{0,1:T(8,128)S(1)}, u32[]{:S(2)}, u32[]{:S(2)}) collective-permute-start(f32[1024,128]{0,1:T(8,128)S(1)} %convolution_bitcast_fusion.3), channel_id=1, source_target_pairs={{0,32},{16,48},{32,0},{48,16},{64,96},{80,112},{96,64},{112,80},{1... | collective-permute-start | bytes 1572872 | tf_op jit(solution)/shard_map/ppermute | solution.py:26
  412.0 29.2 %collective-permute-start.11 = (f32[128,768]{1,0:T(8,128)S(1)}, f32[128,768]{1,0:T(8,128)}, u32[]{:S(2)}, u32[]{:S(2)}) collective-permute-start(f32[128,768]{1,0:T(8,128)S(1)} %convolution_bitcast_fusion.13), channel_id=1, source_target_pairs={{0,1},{1,0},{2,3},{3,2},{4,5},{5,4},{6,7},{7,6},{8,9},{9,8},{10,11... | collective-permute-start | bytes 1179656 | tf_op jit(solution)/shard_map/ppermute | solution.py:26
  417.0 24.1 %copy-start.9 = (f32[256,128]{1,0:T(8,128)}, f32[256,128]{1,0:T(8,128)S(1)}, u32[]{:S(2)}) copy-start(f32[256,128]{1,0:T(8,128)S(1)} %fusion.203) | copy-start | bytes 393220
  442.2 26.2 %copy-start.4 = (f32[256,128]{1,0:T(8,128)S(1)}, f32[256,128]{1,0:T(8,128)}, u32[]{:S(2)}) copy-start(f32[256,128]{1,0:T(8,128)} %copy-done.3) | copy-start | bytes 393220
  442.8 26.2 %copy-start.16 = (f32[1,128,128]{1,2,0:T(8,128)S(1)}, f32[1,128,128]{1,2,0:T(8,128)}, u32[]{:S(2)}) copy-start(f32[1,128,128]{1,2,0:T(8,128)} %copy-done.15) | copy-start | bytes 196612
  444.2 11.7 %collective-permute-start.12 = (f32[128,768]{1,0:T(8,128)S(1)}, f32[128,768]{1,0:T(8,128)S(1)}, u32[]{:S(2)}, u32[]{:S(2)}) collective-permute-start(f32[128,768]{1,0:T(8,128)S(1)} %fusion.91), channel_id=1, source_target_pairs={{0,2},{1,3},{2,0},{3,1},{4,6},{5,7},{6,4},{7,5},{8,10},{9,11},{10,... | collective-permute-start | bytes 1179656 | tf_op jit(solution)/shard_map/ppermute | solution.py:26
  449.7 30.6 %copy-start.6 = (f32[256,128]{1,0:T(8,128)S(1)}, f32[256,128]{1,0:T(8,128)}, u32[]{:S(2)}) copy-start(f32[256,128]{1,0:T(8,128)} %copy-done.5) | copy-start | bytes 393220
  451.2 13.5 %collective-permute-start.10 = (f32[1024,128]{0,1:T(8,128)S(1)}, f32[1024,128]{0,1:T(8,128)S(1)}, u32[]{:S(2)}, u32[]{:S(2)}) collective-permute-start(f32[1024,128]{0,1:T(8,128)S(1)} %convolution_bitcast_fusion.1), channel_id=1, source_target_pairs={{0,64},{16,80},{32,96},{48,112},{64,0},{80,16},{96,32},{112,48},{1... | collective-permute-start | bytes 1572872 | tf_op jit(solution)/shard_map/ppermute | solution.py:26
  457.9 40.9 %copy-start.8 = (f32[256,128]{1,0:T(8,128)S(1)}, f32[256,128]{1,0:T(8,128)}, u32[]{:S(2)}) copy-start(f32[256,128]{1,0:T(8,128)} %copy-done.7) | copy-start | bytes 393220
  458.0 10.4 %collective-permute-start.13 = (f32[128,768]{1,0:T(8,128)S(1)}, f32[128,768]{1,0:T(8,128)S(1)}, u32[]{:S(2)}, u32[]{:S(2)}) collective-permute-start(f32[128,768]{1,0:T(8,128)S(1)} %fusion.86), channel_id=1, source_target_pairs={{0,4},{1,5},{2,6},{3,7},{4,0},{5,1},{6,2},{7,3},{8,12},{9,13},{10,... | collective-permute-start | bytes 1179656 | tf_op jit(solution)/shard_map/ppermute | solution.py:26
  464.8 34.6 %copy-start.19 = (f32[1,128,128]{1,2,0:T(8,128)S(1)}, f32[1,128,128]{1,2,0:T(8,128)}, u32[]{:S(2)}) copy-start(f32[1,128,128]{1,2,0:T(8,128)} %copy-done.18) | copy-start | bytes 196612
  465.9 47.3 %copy-start.10 = (f32[256,128]{1,0:T(8,128)S(1)}, f32[256,128]{1,0:T(8,128)}, u32[]{:S(2)}) copy-start(f32[256,128]{1,0:T(8,128)} %copy-done.9) | copy-start | bytes 393220
  468.4 45.4 %copy-start.20 = (f32[1,128,128]{1,2,0:T(8,128)S(1)}, f32[1,128,128]{1,2,0:T(8,128)}, u32[]{:S(2)}) copy-start(f32[1,128,128]{1,2,0:T(8,128)} %custom-call.37) | copy-start | bytes 196612
  469.6 9.6 %collective-permute-start.14 = (f32[128,768]{1,0:T(8,128)S(1)}, f32[128,768]{1,0:T(8,128)}, u32[]{:S(2)}, u32[]{:S(2)}) collective-permute-start(f32[128,768]{1,0:T(8,128)S(1)} %fusion.81), channel_id=1, source_target_pairs={{0,8},{1,9},{2,10},{3,11},{4,12},{5,13},{6,14},{7,15},{8,0},{9,1},... | collective-permute-start | bytes 1179656 | tf_op jit(solution)/shard_map/ppermute | solution.py:26
  482.2 15.5 %collective-permute-start.15 = (f32[128,768]{1,0:T(8,128)S(1)}, f32[128,768]{1,0:T(8,128)}, u32[]{:S(2)}, u32[]{:S(2)}) collective-permute-start(f32[128,768]{1,0:T(8,128)S(1)} %fusion.76), channel_id=1, source_target_pairs={{0,16},{16,0},{32,48},{48,32},{64,80},{80,64},{96,112},{112,96},{1... | collective-permute-start | bytes 1179656 | tf_op jit(solution)/shard_map/ppermute | solution.py:26
  500.0 12.2 %collective-permute-start.16 = (f32[128,768]{1,0:T(8,128)S(1)}, f32[128,768]{1,0:T(8,128)}, u32[]{:S(2)}, u32[]{:S(2)}) collective-permute-start(f32[128,768]{1,0:T(8,128)S(1)} %fusion.71), channel_id=1, source_target_pairs={{0,32},{16,48},{32,0},{48,16},{64,96},{80,112},{96,64},{112,80},{1... | collective-permute-start | bytes 1179656 | tf_op jit(solution)/shard_map/ppermute | solution.py:26
  514.4 12.0 %collective-permute-start.17 = (f32[128,768]{1,0:T(8,128)S(1)}, f32[128,768]{1,0:T(8,128)S(1)}, u32[]{:S(2)}, u32[]{:S(2)}) collective-permute-start(f32[128,768]{1,0:T(8,128)S(1)} %fusion.66), channel_id=1, source_target_pairs={{0,64},{16,80},{32,96},{48,112},{64,0},{80,16},{96,32},{112,48},{1... | collective-permute-start | bytes 1179656 | tf_op jit(solution)/shard_map/ppermute | solution.py:26
  (7 other events, 72.1 us)
where the time goes:
time: 539 us; the launch traced here: 529 us
  other arithmetic  181 us (34%)
  matrix products  130 us (24%)
  local copies, waits for them, and re-layouts  116 us (22%)
  waiting for transfers between devices  49.2 us (9%)
  starting transfers between devices  42.5 us (8%)
  between operations  10.7 us (2%)
    another operation x21, other arithmetic, merge_pair(): factor = jnp.linalg.cholesky(inner_gram)  86.7 us
    dot_general x6, matrix products, near_field(): jnp.einsum('ijab,ijbr->ijar', near_blocks[:, :, position], near_rows, pre...  81.2 us
    another operation x14, other arithmetic, merge_pair(): lax.linalg.triangular_solve(factor, sketched.T, left_side=True, lower=True)  73.9 us
    gather x6, local copies, waits for them, and re-layouts, near_field(): near_rows = extended[row_base + stencil // 3, col_base + stencil % 3]  66.1 us
    ppermute x14, waiting for transfers between devices, from_partner(): return lax.ppermute(value, axis, pairs)  41.8 us
    ppermute x14, starting transfers between devices, from_partner(): return lax.ppermute(value, axis, pairs)  32.6 us
    unnamed x52, local copies, waits for them, and re-layouts  32 us
    dot_general x7, matrix products, merge_pair(): sketched = jnp.dot(stacked, sketch, precision=highest)  11.8 us
  transfers between devices with their start and end apart: 18, of which 9 were waited for; matrix products, arithmetic and copies ran while one was open for 78% of the time, Pallas kernels for 0%

commit v1 on v0

v1 whole, which is shorter than its diff:
```python
import functools

import jax
import jax.numpy as jnp
from jax import lax
from jax.experimental import pallas as pl
from jax.experimental.pallas import tpu as pltpu
from jax.sharding import PartitionSpec as P

MESH = pl.DeviceIdType.MESH
highest = lax.Precision.HIGHEST
f32 = jnp.float32
LEVELS = 7


def dot_nn(a, b):
    return lax.dot_general(a, b, (((1,), (0,)), ((), ())), precision=highest, preferred_element_type=f32)


def dot_tn(a, b):
    return lax.dot_general(a, b, (((0,), (0,)), ((), ())), precision=highest, preferred_element_type=f32)


def dot_nt(a, b):
    return lax.dot_general(a, b, (((1,), (1,)), ((), ())), precision=highest, preferred_element_type=f32)


def tile(x):
    return jnp.broadcast_to(x, (8, 128))


def cholesky_inverse(gram, out_ref):
    groups = 16
    row = lax.broadcasted_iota(jnp.int32, (8, 128), 0)
    lane = lax.broadcasted_iota(jnp.int32, (8, 128), 1)
    left = [gram[8 * g : 8 * g + 8, :] for g in range(groups)]
    right = [jnp.where(lane == row + 8 * g, 1.0, 0.0).astype(f32) for g in range(groups)]
    for b in range(groups):
        base = 8 * b
        last = b == groups - 1
        cols = [[tile(left[g][:, base + k : base + k + 1]) for k in range(8)] for g in range(b, groups)]
        d = [[tile(cols[0][k][i : i + 1, :]) for k in range(i + 1)] for i in range(8)]
        low = [[None] * 8 for _ in range(8)]
        inv = [[None] * 8 for _ in range(8)]
        for k in range(8):
            scale = lax.rsqrt(d[k][k])
            for i in range(k + 1, 8):
                low[i][k] = d[i][k] * scale
            for m in range(k + 1, 8):
                for i in range(m, 8):
                    d[i][m] = d[i][m] - low[i][k] * low[m][k]
            inv[k][k] = scale
            for j in range(k):
                s = low[k][j] * inv[j][j]
                for q in range(j + 1, k):
                    s = s + low[k][q] * inv[q][j]
                inv[k][j] = -(scale * s)

        def solved(panel):
            up = []
            for i in range(8):
                s = inv[i][0] * panel[0]
                for k in range(1, i + 1):
                    s = s + inv[i][k] * panel[k]
                up.append(s)
            return up

        def solved_again(up):
            full = []
            for k in range(8):
                s = inv[k][k] * up[k]
                for i in range(k + 1, 8):
                    s = s + inv[i][k] * up[i]
                full.append(s)
            return full

        up_right = solved([tile(right[b][k : k + 1, :]) for k in range(8)])
        for i in range(8):
            out_ref[base + i : base + i + 1, :] = up_right[i][0:1, :]
        if last:
            break
        full_left = solved_again(solved([tile(left[b][k : k + 1, :]) for k in range(8)]))
        full_right = solved_again(up_right)
        for g in range(b + 1, groups):
            c = cols[g - b]
            drop_left = c[0] * full_left[0]
            drop_right = c[0] * full_right[0]
            for k in range(1, 8):
                drop_left = drop_left + c[k] * full_left[k]
                drop_right = drop_right + c[k] * full_right[k]
            left[g] = left[g] - drop_left
            right[g] = right[g] - drop_right


def flip(index, bit):
    return index + bit - 2 * bit * ((index // bit) % 2)


def tree_kernel(
    leaf, sketch, keys, path_out, root_out,
    mine, other, w_mine, w_other, halves, gram_send, gram_recv, gram, linv, path, before, swap,
    leaf_local, leaf_send, leaf_recv, y_send, y_recv, w_send, w_recv, g_send, g_recv, s_send, s_recv,
):
    u = lax.axis_index("pu")
    v = lax.axis_index("pv")
    core = u % 2
    y = u // 2
    x0 = v % 2
    u_core = flip(u, 1)
    v_next = flip(v, 1)
    partners = {1: (u, flip(v, 2)), 2: (u, flip(v, 4)), 3: (u, flip(v, 8)), 4: (u, v_next), 5: (flip(u, 2), v), 6: (flip(u, 4), v)}
    barrier = pltpu.get_barrier_semaphore()
    peers = list(partners.values()) + [(u_core, v), (u_core, v_next)]
    for peer in peers:
        pl.semaphore_signal(barrier, inc=1, device_id=peer, device_id_type=MESH)
    pl.semaphore_wait(barrier, len(peers))

    def leaf_copy(part, slot_ref, to, slot):
        return pltpu.make_async_remote_copy(
            src_ref=leaf.at[:, part], dst_ref=slot_ref.at[0], send_sem=leaf_send.at[part],
            recv_sem=leaf_recv.at[slot], device_id=to, device_id_type=MESH,
        )

    slots = (mine, other)
    for c in range(2):
        for x in range(2):
            @pl.when((core == c) & (x0 == x))
            def _(c=c, x=x):
                if c == x:
                    local = pltpu.make_async_copy(leaf.at[:, c], slots[x].at[0], leaf_local)
                    local.start()
                    leaf_copy(1 - c, slots[x], (u_core, v), x).start()
                    local.wait()
                else:
                    leaf_copy(c, slots[x], (u, v_next), x).start()
                    leaf_copy(1 - c, slots[x], (u_core, v_next), x).start()

    key = keys[...]
    rows = lax.broadcasted_iota(jnp.int32, (8, 16), 0)
    cols = lax.broadcasted_iota(jnp.int32, (8, 16), 1)
    host_row = 2 * y + x0

    def least(mask):
        return jnp.min(jnp.min(jnp.where(mask, key, 1 << 20), axis=1, keepdims=True), axis=0, keepdims=True)

    here = rows == host_row
    even = v - x0
    pairs = [(here & (cols == even), here & (cols == even + 1))]
    for bit in (2, 4, 8):
        pairs.append((here & (cols // bit == v // bit), here & (cols // bit == flip(v, bit) // bit)))
    pairs.append((here, rows == 2 * y + 1 - x0))
    for bit in (2, 4):
        pairs.append((rows // bit == u // bit, rows // bit == flip(u, bit) // bit))
    first = sketch[0:128, :]
    second = sketch[128:256, :]
    for t, (own, sibling) in enumerate(pairs):
        leads = jnp.broadcast_to((least(own) < least(sibling)).astype(f32), (128, 128)) > 0.5
        halves[t] = jnp.where(leads, first, second)
        if t == 0:
            w_mine[0] = halves[0]
            w_other[0] = jnp.where(leads, second, first)
    diag = lax.broadcasted_iota(jnp.int32, (128, 128), 0) == lax.broadcasted_iota(jnp.int32, (128, 128), 1)
    before[...] = jnp.where(diag, 1.0, 0.0).astype(f32)

    for c in range(2):
        for x in range(2):
            @pl.when((core == c) & (x0 == x))
            def _(c=c, x=x):
                if c == x:
                    leaf_copy(1 - c, slots[x], (u_core, v), x).wait_send()
                    leaf_copy(0, slots[1 - x], (u_core, v), 1 - x).wait_recv()
                else:
                    for part in range(2):
                        leaf_copy(part, slots[x], (u_core, v), x).wait_send()
                    for slot in range(2):
                        leaf_copy(0, slots[slot], (u_core, v), slot).wait_recv()

    def y_copy(t, to):
        return pltpu.make_async_remote_copy(
            src_ref=mine.at[t + 1], dst_ref=other.at[t + 1], send_sem=y_send.at[t], recv_sem=y_recv.at[t],
            device_id=to, device_id_type=MESH,
        )

    def w_copy(t, to):
        return pltpu.make_async_remote_copy(
            src_ref=w_mine.at[t + 1], dst_ref=w_other.at[t + 1], send_sem=w_send.at[t], recv_sem=w_recv.at[t],
            device_id=to, device_id_type=MESH,
        )

    def g_copy(t, kind):
        return pltpu.make_async_remote_copy(
            src_ref=gram_send.at[t, kind], dst_ref=gram_recv.at[t, kind], send_sem=g_send.at[t, kind],
            recv_sem=g_recv.at[t, kind], device_id=(u_core, v), device_id_type=MESH,
        )

    def swap_copy():
        return pltpu.make_async_remote_copy(
            src_ref=path, dst_ref=swap, send_sem=s_send, recv_sem=s_recv,
            device_id=(u_core, v_next), device_id_type=MESH,
        )

    def merge(t, carry):
        for r in range(4):
            part = (t, r)
            mine[t + 1, r] = dot_nn(mine[part], w_mine[t]) + dot_nn(other[part], w_other[t])
        for step in range(LEVELS - 1):
            @pl.when(t == step)
            def _(step=step):
                y_copy(step, partners[step + 1]).start()
        merged = mine[t + 1].reshape(512, 128)
        part_gram = dot_tn(merged, merged)
        gram_send[t, 0] = part_gram
        g_copy(t, 0).start()
        part_cross = dot_tn(merged, mine[t].reshape(512, 128))
        gram_send[t, 1] = part_cross
        gram[1] = part_cross

        @pl.when(t == 0)
        def _():
            second_cross = dot_tn(merged, other[t].reshape(512, 128))

            @pl.when(core == 0)
            def _():
                gram_send[t, 1] = second_cross

            @pl.when(core == 1)
            def _():
                gram[1] = second_cross

        g_copy(t, 1).start()
        g_copy(t, 0).wait()
        gram[0] = part_gram + gram_recv[t, 0]
        cholesky_inverse(gram.at[0], linv)
        factor = linv[...]

        @pl.when(t < LEVELS - 1)
        def _():
            w_mine[t + 1] = dot_tn(factor, halves[t + 1])

        for step in range(LEVELS - 1):
            @pl.when(t == step)
            def _(step=step):
                w_copy(step, partners[step + 1]).start()

        g_copy(t, 1).wait()
        path[...] = dot_nn(factor, dot_nn(gram[1] + gram_recv[t, 1], before[...]))

        @pl.when((t == 4) & (core != x0))
        def _():
            swap_copy().start()
            swap_copy().wait()
            path[...] = swap[...]

        before[...] = dot_tn(factor, path[...])

        @pl.when(t < LEVELS - 1)
        def _():
            y_copy(t, (u_core, v)).wait()
            w_copy(t, (u_core, v)).wait()

        return carry

    lax.fori_loop(0, LEVELS, merge, 0)
    path_out[...] = path[...]
    root_out[...] = dot_nt(mine[LEVELS, y], linv[...])


def tree(far_left, sketch, keys):
    square = jax.ShapeDtypeStruct((128, 128), f32)
    vmem = pl.BlockSpec(memory_space=pltpu.VMEM)
    dma = pltpu.SemaphoreType.DMA
    return pl.pallas_call(
        tree_kernel,
        out_shape=(square, square),
        in_specs=[pl.BlockSpec(memory_space=pl.ANY), vmem, vmem],
        out_specs=(vmem, vmem),
        scratch_shapes=[
            pltpu.VMEM((LEVELS + 1, 4, 128, 128), f32),
            pltpu.VMEM((LEVELS + 1, 4, 128, 128), f32),
            pltpu.VMEM((LEVELS + 1, 128, 128), f32),
            pltpu.VMEM((LEVELS + 1, 128, 128), f32),
            pltpu.VMEM((LEVELS, 128, 128), f32),
            pltpu.VMEM((LEVELS, 2, 128, 128), f32),
            pltpu.VMEM((LEVELS, 2, 128, 128), f32),
            pltpu.VMEM((2, 128, 128), f32),
            pltpu.VMEM((128, 128), f32),
            pltpu.VMEM((128, 128), f32),
            pltpu.VMEM((128, 128), f32),
            pltpu.VMEM((128, 128), f32),
            dma, dma((2,)), dma((2,)),
            dma((LEVELS,)), dma((LEVELS,)), dma((LEVELS,)), dma((LEVELS,)),
            dma((LEVELS, 2)), dma((LEVELS, 2)), dma, dma,
        ],
        compiler_params=pltpu.CompilerParams(collective_id=0, has_side_effects=True, vmem_limit_bytes=32 * 2**20),
        cost_estimate=pl.CostEstimate(flops=10**10, bytes_accessed=2**20, transcendentals=0),
        name="tree",
    )(far_left.reshape(4, 2, 128, 128), sketch, keys)


def near_block(i, j, links, ext, near):
    where = []
    for s in range(6):
        e = links[i, 6 * j + s]
        down = (e * 11) // 32
        where.append((jnp.where(e < 9, i + down, 8), jnp.where(e < 9, j + e - 3 * down, 0)))
    lhs = jnp.concatenate([near[i, j, s] for s in range(6)], axis=1)
    rhs = jnp.concatenate([ext[a, b] for a, b in where], axis=0)
    summed = jnp.dot(lhs, rhs, preferred_element_type=f32)
    return (ext[i + 1, j + 1].astype(f32) + summed).astype(jnp.bfloat16)


def near_kernel(
    links, density, low, high, west, east, near_hbm, right_hbm, path, corrected, out_ref,
    ext, near, right, out, coef, sem, halo_sem, out_sem,
):
    bands = []
    for r in range(6):
        band = [
            pltpu.make_async_copy(density.at[r], ext.at[r + 1, 1:7], sem.at[r, 0]),
            pltpu.make_async_copy(near_hbm.at[r], near.at[r], sem.at[r, 1]),
            pltpu.make_async_copy(right_hbm.at[r], right.at[r], sem.at[r, 2]),
        ]
        for copy in band:
            copy.start()
        bands.append(band)
    halo = [
        pltpu.make_async_copy(low, ext.at[0, 1:7], halo_sem.at[0]),
        pltpu.make_async_copy(high, ext.at[7, 1:7], halo_sem.at[1]),
        pltpu.make_async_copy(west, ext.at[0:8, 0], halo_sem.at[2]),
        pltpu.make_async_copy(east, ext.at[0:8, 7], halo_sem.at[3]),
    ]
    for copy in halo:
        copy.start()
    ext[8, 0] = jnp.zeros((128, 768), jnp.bfloat16)
    coef[...] = jnp.zeros_like(coef)
    for copy in halo:
        copy.wait()
    for band in bands:
        for copy in band:
            copy.wait()

    def out_copy(i):
        return pltpu.make_async_copy(out.at[i], corrected.at[i], out_sem.at[i])

    def line(i, carry):
        def pair(m, inner):
            j = 2 * m
            done = []
            for q in range(2):
                block = near_block(i, j + q, links, ext, near)
                out[i, j + q] = block
                done.append(block)
            lhs = jnp.concatenate([right[i, j], right[i, j + 1]], axis=0)
            coef[...] += lax.dot_general(
                lhs, jnp.concatenate(done, axis=0), (((0,), (0,)), ((), ())), preferred_element_type=f32
            )
            return inner

        lax.fori_loop(0, 3, pair, 0)
        out_copy(i).start()
        return carry

    lax.fori_loop(0, 6, line, 0)
    out_ref[...] = lax.dot_general(coef[...], path[...], (((0,), (1,)), ((), ())), precision=highest, preferred_element_type=f32)
    for i in range(6):
        out_copy(i).wait()


def near_field(links, density, low, high, west, east, near_blocks, far_right, path):
    anywhere = pl.BlockSpec(memory_space=pl.ANY)
    vmem = pl.BlockSpec(memory_space=pltpu.VMEM)
    dma = pltpu.SemaphoreType.DMA
    return pl.pallas_call(
        near_kernel,
        out_shape=(jax.ShapeDtypeStruct((6, 6, 128, 768), jnp.bfloat16), jax.ShapeDtypeStruct((768, 128), f32)),
        in_specs=[pl.BlockSpec(memory_space=pltpu.SMEM)] + [anywhere] * 7 + [vmem],
        out_specs=(anywhere, vmem),
        scratch_shapes=[
            pltpu.VMEM((9, 8, 128, 768), jnp.bfloat16),
            pltpu.VMEM((6, 6, 6, 128, 128), jnp.bfloat16),
            pltpu.VMEM((6, 6, 128, 128), jnp.bfloat16),
            pltpu.VMEM((6, 6, 128, 768), jnp.bfloat16),
            pltpu.VMEM((128, 768), f32),
            dma((6, 3)), dma((4,)), dma((6,)),
        ],
        compiler_params=pltpu.CompilerParams(vmem_limit_bytes=48 * 2**20),
        name="near",
    )(links.reshape(6, 36), density, low, high, west, east, near_blocks, far_right, path)


def gather_kernel(term, root, out_ref, from_row, row_sum, from_col, row_send, row_recv, col_send, col_recv):
    u = lax.axis_index("pu")
    v = lax.axis_index("pv")
    barrier = pltpu.get_barrier_semaphore()
    for d in range(1, 16):
        pl.semaphore_signal(barrier, inc=1, device_id=(u, (v + d) % 16), device_id_type=MESH)
    for d in range(1, 8):
        pl.semaphore_signal(barrier, inc=1, device_id=((u + d) % 8, v), device_id_type=MESH)
    pl.semaphore_wait(barrier, 22)
    copies = []
    for d in range(1, 16):
        to = (v + d) % 16
        copy = pltpu.make_async_remote_copy(
            src_ref=term.at[to], dst_ref=from_row.at[d], send_sem=row_send.at[d], recv_sem=row_recv.at[d],
            device_id=(u, to), device_id_type=MESH,
        )
        copy.start()
        copies.append(copy)
    total = term[v]
    for d in range(1, 16):
        copies[d - 1].wait()
        total = total + from_row[d]
    row_sum[...] = total
    copies = []
    for d in range(1, 8):
        copy = pltpu.make_async_remote_copy(
            src_ref=row_sum, dst_ref=from_col.at[d], send_sem=col_send.at[d], recv_sem=col_recv.at[d],
            device_id=((u + d) % 8, v), device_id_type=MESH,
        )
        copy.start()
        copies.append(copy)
    for d in range(1, 8):
        copies[d - 1].wait()
        total = total + from_col[d]
    out_ref[...] = dot_nt(root[...], total)


def gathered(term, root):
    vmem = pl.BlockSpec(memory_space=pltpu.VMEM)
    dma = pltpu.SemaphoreType.DMA
    return pl.pallas_call(
        gather_kernel,
        out_shape=jax.ShapeDtypeStruct((128, 48), f32),
        in_specs=[vmem, vmem],
        out_specs=vmem,
        scratch_shapes=[
            pltpu.VMEM((16, 48, 128), f32), pltpu.VMEM((48, 128), f32), pltpu.VMEM((8, 48, 128), f32),
            dma((16,)), dma((16,)), dma((8,)), dma((8,)),
        ],
        compiler_params=pltpu.CompilerParams(collective_id=1, has_side_effects=True, vmem_limit_bytes=16 * 2**20),
        name="gather",
    )(term.reshape(16, 48, 128), root)


def from_sides(block, axis, dim):
    count = lax.axis_size(axis)
    forward = [(i, i + 1) for i in range(count - 1)]
    backward = [(target, source) for source, target in forward]
    low = lax.ppermute(lax.slice_in_dim(block, block.shape[dim] - 1, None, axis=dim), axis, forward)
    high = lax.ppermute(lax.slice_in_dim(block, 0, 1, axis=dim), axis, backward)
    return low, high


def per_device(density, near_blocks, neighbours, far_right, far_left, sketch, patch_order):
    low, high = from_sides(density, "pu", 0)
    edges = jnp.concatenate([low[:, ::5], density[:, ::5], high[:, ::5]], axis=0)
    west, east = from_sides(edges, "pv", 1)
    path, root = tree(far_left, sketch, patch_order.reshape(8, 16))
    corrected, term = near_field(
        neighbours, density, low[0], high[0], west[:, 0], east[:, 0], near_blocks, far_right, path
    )
    return (corrected, gathered(term, root))


def solution(mesh):
    in_specs = (
        P("pu", "pv", None, None),
        P("pu", "pv", None, None, None),
        P("pu", "pv", None),
        P("pu", "pv", None, None),
        P("pu", "pv", None, None),
        P(),
        P(),
    )
    out_specs = (P("pu", "pv", None, None), P("pu", "pv"))
    return jax.shard_map(
        per_device, mesh=mesh, in_specs=in_specs, out_specs=out_specs, check_vma=False
    )
```

time: 539 us -> 192 us (0.36); the launches traced: 529 us -> 191 us
  other arithmetic: 181 us -> 1.77 us
  Pallas kernels: 0 us -> 158 us
  matrix products: 130 us -> 0 us
  local copies, waits for them, and re-layouts: 116 us -> 4.6 us
  waiting for transfers between devices: 49.2 us -> 13.1 us
  starting transfers between devices: 42.5 us -> 12.9 us
  between operations: 10.7 us -> 0.76 us
    another operation x35 -> x0, other arithmetic: 161 us -> none  [the longest x21 86.7 us: merge_pair(): factor = jnp.linalg.cholesky(inner_gram)]
    pallas_call x0 -> x3, Pallas kernels: none -> 158 us  [the longest x1 123 us: tree(): pl.pallas_call(tree_kernel, out_shape=(square, square), in_specs=[pl.Bloc...]
    dot_general x43 -> x0, matrix products: 118 us -> none  [the longest x6 81.2 us: near_field(): jnp.einsum('ijab,ijbr->ijar', near_blocks[:, :, position], near_rows, pre...]
    gather x6 -> x0, local copies, waits for them, and re-layouts: 66.1 us -> none  [near_field(): near_rows = extended[row_base + stencil // 3, col_base + stencil % 3]]
    ppermute x18 -> x4, waiting for transfers between devices: 49.2 us -> 13.1 us  [the longest x2 12.3 us: from_sides(): high = lax.ppermute(lax.slice_in_dim(block, 0, 1, axis=dim), axis, backward)]
    ppermute x18 -> x4, starting transfers between devices: 42.5 us -> 12.9 us  [the longest x2 8.33 us: from_sides(): lax.ppermute(lax.slice_in_dim(block, block.shape[dim] - 1, None, axis=dim...]
    unnamed x52 -> x12, local copies, waits for them, and re-layouts: 32 us -> 2.5 us
    another operation x14 -> x0, matrix products: 11.5 us -> none  [the longest x7 6.14 us: merge_pair(): lax.linalg.triangular_solve(factor, jnp.dot(reduced, coeff_pairs, precisi...]
  transfers between devices with their start and end apart: 18 -> 4, of which waited for: 9 -> 2; matrix products, arithmetic and copies ran while one was open for 78% -> 0% of each run, Pallas kernels for 0% -> 64%
where the time goes in v1:
time: 192 us; the launch traced here: 191 us
  Pallas kernels  158 us (82%)
  waiting for transfers between devices  13.1 us (7%)
  starting transfers between devices  12.9 us (7%)
  local copies, waits for them, and re-layouts  4.6 us (2%)
    pallas_call x1, Pallas kernels, tree(): pl.pallas_call(tree_kernel, out_shape=(square, square), in_specs=[pl.Bloc...  123 us
    pallas_call x1, Pallas kernels, near_field(): pl.pallas_call(near_kernel, out_shape=(jax.ShapeDtypeStruct((6, 6, 128, 7...  20 us
    pallas_call x1, Pallas kernels, gathered(): pl.pallas_call(gather_kernel, out_shape=jax.ShapeDtypeStruct((128, 48), f...  15.3 us
    ppermute x2, waiting for transfers between devices, from_sides(): high = lax.ppermute(lax.slice_in_dim(block, 0, 1, axis=dim), axis, backward)  12.3 us
    ppermute x2, starting transfers between devices, from_sides(): lax.ppermute(lax.slice_in_dim(block, block.shape[dim] - 1, None, axis=dim...  8.33 us
    ppermute x2, starting transfers between devices, from_sides(): high = lax.ppermute(lax.slice_in_dim(block, 0, 1, axis=dim), axis, backward)  4.61 us
  transfers between devices with their start and end apart: 4, of which 2 were waited for; matrix products, arithmetic and copies ran while one was open for 0% of the time, Pallas kernels for 64%

profile of v1, /device:TPU:1, one launch (start us, length us, event | category | flops | bytes accessed | tf_op | source)
XLA Modules:
  0.0 191.5 jit_solution(5111154114164635038)
XLA Ops:
  0.6 1.8 slice_bitcast_fusion
  2.4 3.3 %collective-permute-start.1 = (bf16[1,6,128,768]{3,2,0,1:T(8,128)(2,1)S(1)}, bf16[1,6,128,768]{3,2,0,1:T(8,128)(2,1)S(1)}, u32[]{:S(2)}, u32[]{:S(2)}) collective-permute-start(bf16[1,6,128,768]{3,2,0,1:T(8,128)(2,1)S(1)} %get-tuple-element.12), channel_id=1, source_target_pairs={{16,0},{32,16},{48,32},{64,48},{80,64},{96,80},{112,96},{17,1},{33... | collective-permute-start | bytes 3538952 | tf_op jit(solution)/shard_map/ppermute | solution.py:450
  5.8 3.2 %collective-permute-start = (bf16[1,6,128,768]{3,2,0,1:T(8,128)(2,1)S(1)}, bf16[1,6,128,768]{3,2,0,1:T(8,128)(2,1)S(1)}, u32[]{:S(2)}, u32[]{:S(2)}) collective-permute-start(bf16[1,6,128,768]{3,2,0,1:T(8,128)(2,1)S(1)} %get-tuple-element.13), channel_id=1, source_target_pairs={{0,16},{16,32},{32,48},{48,64},{64,80},{80,96},{96,112},{1,17},{17... | collective-permute-start | bytes 3538952 | tf_op jit(solution)/shard_map/ppermute | solution.py:449
  8.9 12.3 %collective-permute-done.1 = bf16[1,6,128,768]{3,2,0,1:T(8,128)(2,1)S(1)} collective-permute-done((bf16[1,6,128,768]{3,2,0,1:T(8,128)(2,1)S(1)}, bf16[1,6,128,768]{3,2,0,1:T(8,128)(2,1)S(1)}, u32[]{:S(2)}, u32[]{:S(2)}) %collective-permute-start.1) | collective-permute-done | bytes 1179680 | tf_op jit(solution)/shard_map/ppermute | solution.py:450
  21.3 0.8 collective-permute-done
  22.1 1.8 pad_maximum_fusion
  23.9 0.0 copy-start.3
  23.9 0.0 copy-start.4
  23.9 0.0 copy-start.1
  23.9 0.0 copy-start.2
  23.9 1.9 fusion
  25.8 1.3 collective-permute-start.3
  27.1 5.1 %collective-permute-start.2 = (bf16[8,1,128,768]{3,2,0,1:T(8,128)(2,1)}, bf16[8,1,128,768]{3,2,0,1:T(8,128)(2,1)}, u32[]{:S(2)}, u32[]{:S(2)}) collective-permute-start(bf16[8,1,128,768]{3,2,0,1:T(8,128)(2,1)} %get-tuple-element.15), channel_id=1, source_target_pairs={{0,1},{1,2},{2,3},{3,4},{4,5},{5,6},{6,7},{7,8},{8,9},{9,10},{10,1... | collective-permute-start | bytes 4718600 | tf_op jit(solution)/shard_map/ppermute | solution.py:449
  32.3 0.0 copy-done.3
  32.3 0.1 reshape.16.links
  32.3 0.0 copy-done.4
  32.3 0.1 reshape.18.keys
  32.4 0.0 copy-done.1
  32.4 0.0 copy-done.2
  32.4 0.0 copy-start
  32.4 123.0 %tree.1 = (f32[128,128]{1,0:T(8,128)S(1)}, f32[128,128]{1,0:T(8,128)S(1)}) custom-call(f32[4,2,128,128]{3,2,1,0:T(8,128)S(1)} %bitcast.13, f32[256,128]{1,0:T(8,128)S(1)} %copy-done.2, s32[8,16]{1,0:T(8,128)S(1)} %reshape.18.keys), custom_call_target="tpu_custom_call" | custom-call | flops 10000000000 | bytes 1048576 | tf_op jit(solution)/shard_map/tree/pallas_call | solution.py:272
  155.4 0.0 collective-permute-done.3
  155.4 0.0 collective-permute-done.2
  155.4 0.0 copy-done
  155.4 20.0 %near.1 = (bf16[6,6,128,768]{3,2,1,0:T(8,128)(2,1)}, f32[768,128]{1,0:T(8,128)S(1)}) custom-call(s32[6,36]{1,0:T(8,128)S(1)} %reshape.16.links, bf16[6,6,128,768]{3,2,1,0:T(8,128)(2,1)} %density.1, bf16[6,128,768]{2,1,0:T(8,128)(2,1)S(1)} %bitcast.11, bf16[6,128,768]{2,1,0:T(8,128)(2,1)S(1)} %bitcast.10, bf16[8,128,768]{2,1,0:T(8,128)(2,1)} %bitcast.2.west, ...), custom_call_target="tpu_custom_call" | custom-call | tf_op jit(solution)/shard_map/near/pallas_call | solution.py:373
  175.5 15.3 %gather.1 = f32[128,48]{1,0:T(8,128)S(1)} custom-call(f32[16,48,128]{2,1,0:T(8,128)S(1)} %bitcast.12, f32[128,128]{1,0:T(8,128)S(1)} %get-tuple-element.9.root), custom_call_target="tpu_custom_call" | custom-call | tf_op jit(solution)/shard_map/gather/pallas_call | solution.py:431
  190.8 0.7 copy.12
  (2 shorter events, 0.1 us)
Async XLA Ops:
  2.4 18.9 %collective-permute-start.1 = (bf16[1,6,128,768]{3,2,0,1:T(8,128)(2,1)S(1)}, bf16[1,6,128,768]{3,2,0,1:T(8,128)(2,1)S(1)}, u32[]{:S(2)}, u32[]{:S(2)}) collective-permute-start(bf16[1,6,128,768]{3,2,0,1:T(8,128)(2,1)S(1)} %get-tuple-element.12), channel_id=1, source_target_pairs={{16,0},{32,16},{48,32},{64,48},{80,64},{96,80},{112,96},{17,1},{33... | collective-permute-start | bytes 3538952 | tf_op jit(solution)/shard_map/ppermute | solution.py:450
  5.8 16.3 %collective-permute-start = (bf16[1,6,128,768]{3,2,0,1:T(8,128)(2,1)S(1)}, bf16[1,6,128,768]{3,2,0,1:T(8,128)(2,1)S(1)}, u32[]{:S(2)}, u32[]{:S(2)}) collective-permute-start(bf16[1,6,128,768]{3,2,0,1:T(8,128)(2,1)S(1)} %get-tuple-element.13), channel_id=1, source_target_pairs={{0,16},{16,32},{32,48},{48,64},{64,80},{80,96},{96,112},{1,17},{17... | collective-permute-start | bytes 3538952 | tf_op jit(solution)/shard_map/ppermute | solution.py:449
  23.9 8.4 %copy-start.3 = (s32[6,6,6]{2,1,0:T(8,128)S(1)}, s32[6,6,6]{2,1,0:T(8,128)}, u32[]{:S(2)}) copy-start(s32[6,6,6]{2,1,0:T(8,128)} %param.9) | copy-start | bytes 2596
  23.9 8.4 %copy-start.4 = (s32[128]{0:T(128)S(1)}, s32[128]{0:T(128)}, u32[]{:S(2)}) copy-start(s32[128]{0:T(128)} %param.13) | copy-start | bytes 1540
  23.9 8.5 %copy-start.1 = (f32[1,1,1024,128]{3,2,1,0:T(8,128)S(1)}, f32[1,1,1024,128]{3,2,1,0:T(8,128)}, u32[]{:S(2)}) copy-start(f32[1,1,1024,128]{3,2,1,0:T(8,128)} %param.11) | copy-start | bytes 1572868
  23.9 8.5 %copy-start.2 = (f32[256,128]{1,0:T(8,128)S(1)}, f32[256,128]{1,0:T(8,128)}, u32[]{:S(2)}) copy-start(f32[256,128]{1,0:T(8,128)} %sketch.1) | copy-start | bytes 393220
  25.8 129.6 %collective-permute-start.3 = (bf16[8,1,128,768]{3,2,0,1:T(8,128)(2,1)}, bf16[8,1,128,768]{3,2,0,1:T(8,128)(2,1)}, u32[]{:S(2)}, u32[]{:S(2)}) collective-permute-start(bf16[8,1,128,768]{3,2,0,1:T(8,128)(2,1)} %get-tuple-element.14), channel_id=1, source_target_pairs={{1,0},{2,1},{3,2},{4,3},{5,4},{6,5},{7,6},{8,7},{9,8},{10,9},{11,1... | collective-permute-start | bytes 4718600 | tf_op jit(solution)/shard_map/ppermute | solution.py:450
  27.1 128.3 %collective-permute-start.2 = (bf16[8,1,128,768]{3,2,0,1:T(8,128)(2,1)}, bf16[8,1,128,768]{3,2,0,1:T(8,128)(2,1)}, u32[]{:S(2)}, u32[]{:S(2)}) collective-permute-start(bf16[8,1,128,768]{3,2,0,1:T(8,128)(2,1)} %get-tuple-element.15), channel_id=1, source_target_pairs={{0,1},{1,2},{2,3},{3,4},{4,5},{5,6},{6,7},{7,8},{8,9},{9,10},{10,1... | collective-permute-start | bytes 4718600 | tf_op jit(solution)/shard_map/ppermute | solution.py:449
  32.4 123.0 %copy-start = (bf16[6,6,128,128]{3,2,1,0:T(8,128)(2,1)S(1)}, bf16[6,6,128,128]{3,2,1,0:T(8,128)(2,1)}, u32[]{:S(2)}) copy-start(bf16[6,6,128,128]{3,2,1,0:T(8,128)(2,1)} %right_hbm.1) | copy-start | bytes 3538948

commit v2 on v1

v2 whole, which is shorter than its diff:
```python
import functools

import jax
import jax.numpy as jnp
from jax import lax
from jax.experimental import pallas as pl
from jax.experimental.pallas import tpu as pltpu
from jax.sharding import PartitionSpec as P

MESH = pl.DeviceIdType.MESH
highest = lax.Precision.HIGHEST
f32 = jnp.float32
LEVELS = 7


def dot_nn(a, b):
    return lax.dot_general(a, b, (((1,), (0,)), ((), ())), precision=highest, preferred_element_type=f32)


def dot_tn(a, b):
    return lax.dot_general(a, b, (((0,), (0,)), ((), ())), precision=highest, preferred_element_type=f32)


def dot_nt(a, b):
    return lax.dot_general(a, b, (((1,), (1,)), ((), ())), precision=highest, preferred_element_type=f32)


def tile(x):
    return jnp.broadcast_to(x, (8, 128))


def cholesky_inverse(gram, out_ref):
    groups = 16
    row = lax.broadcasted_iota(jnp.int32, (8, 128), 0)
    lane = lax.broadcasted_iota(jnp.int32, (8, 128), 1)
    left = [gram[8 * g : 8 * g + 8, :] for g in range(groups)]
    right = [jnp.where(lane == row + 8 * g, 1.0, 0.0).astype(f32) for g in range(groups)]
    for b in range(groups):
        base = 8 * b
        last = b == groups - 1
        cols = [[tile(left[g][:, base + k : base + k + 1]) for k in range(8)] for g in range(b, groups)]
        d = [[tile(cols[0][k][i : i + 1, :]) for k in range(i + 1)] for i in range(8)]
        low = [[None] * 8 for _ in range(8)]
        inv = [[None] * 8 for _ in range(8)]
        for k in range(8):
            scale = lax.rsqrt(d[k][k])
            for i in range(k + 1, 8):
                low[i][k] = d[i][k] * scale
            for m in range(k + 1, 8):
                for i in range(m, 8):
                    d[i][m] = d[i][m] - low[i][k] * low[m][k]
            inv[k][k] = scale
            for j in range(k):
                s = low[k][j] * inv[j][j]
                for q in range(j + 1, k):
                    s = s + low[k][q] * inv[q][j]
                inv[k][j] = -(scale * s)

        def solved(panel):
            up = []
            for i in range(8):
                s = inv[i][0] * panel[0]
                for k in range(1, i + 1):
                    s = s + inv[i][k] * panel[k]
                up.append(s)
            return up

        def solved_again(up):
            full = []
            for k in range(8):
                s = inv[k][k] * up[k]
                for i in range(k + 1, 8):
                    s = s + inv[i][k] * up[i]
                full.append(s)
            return full

        up_right = solved([tile(right[b][k : k + 1, :]) for k in range(8)])
        for i in range(8):
            out_ref[base + i : base + i + 1, :] = up_right[i][0:1, :]
        if last:
            break
        full_left = solved_again(solved([tile(left[b][k : k + 1, :]) for k in range(8)]))
        full_right = solved_again(up_right)
        for g in range(b + 1, groups):
            c = cols[g - b]
            drop_left = c[0] * full_left[0]
            drop_right = c[0] * full_right[0]
            for k in range(1, 8):
                drop_left = drop_left + c[k] * full_left[k]
                drop_right = drop_right + c[k] * full_right[k]
            left[g] = left[g] - drop_left
            right[g] = right[g] - drop_right


def flip(index, bit):
    return index + bit - 2 * bit * ((index // bit) % 2)


def near_pair(i, cols, links, source, shift, near, right, out, coef):
    done = []
    for j in cols:
        where = []
        for s in range(6):
            e = links[i, 6 * j + s]
            down = (e * 11) // 32
            across = e - 3 * down
            where.append(
                (jnp.where(e < 9, i + down + shift - 1, 6 + 2 * shift), jnp.where(e < 9, j + across + shift - 1, 0))
            )
        lhs = jnp.concatenate([near[i, j, s] for s in range(6)], axis=1)
        rhs = jnp.concatenate([source[a, b] for a, b in where], axis=0)
        summed = jnp.dot(lhs, rhs, preferred_element_type=f32)
        block = (source[i + shift, j + shift].astype(f32) + summed).astype(jnp.bfloat16)
        out[i, j] = block
        done.append(block)
    lhs = jnp.concatenate([right[i, j] for j in cols], axis=0)
    coef[...] += lax.dot_general(
        lhs, jnp.concatenate(done, axis=0), (((0,), (0,)), ((), ())), preferred_element_type=f32
    )


def solver_kernel(
    links, density, near_hbm, right_hbm, leaf, sketch, keys, corrected, far_out,
    ext, inner, near, right, out, coef,
    mine, other, w_mine, w_other, halves, base, cross_send, cross_recv, cross, gram, linv, path, swap,
    term, from_row, row_sum, from_col,
    load_sem, out_sem, halo_send, halo_recv,
    leaf_local, leaf_send, leaf_recv, y_send, y_recv, w_send, w_recv, c_send, c_recv, g_send, g_recv, s_send, s_recv,
    row_send, row_recv, col_send, col_recv,
):
    u = lax.axis_index("pu")
    v = lax.axis_index("pv")
    core = u % 2
    y = u // 2
    x0 = v % 2
    u_core = flip(u, 1)
    v_next = flip(v, 1)
    partners = {1: (u, flip(v, 2)), 2: (u, flip(v, 4)), 3: (u, flip(v, 8)), 4: (u, v_next), 5: (flip(u, 2), v), 6: (flip(u, 4), v)}
    barrier = pltpu.get_barrier_semaphore()
    peers = list(partners.values()) + [(u_core, v), (u_core, v_next)]
    for du in (7, 0, 1):
        for dv in (15, 0, 1):
            if du or dv:
                peers.append(((u + du) % 8, (v + dv) % 16))
    for peer in peers:
        pl.semaphore_signal(barrier, inc=1, device_id=peer, device_id_type=MESH)
    loads = [
        pltpu.make_async_copy(near_hbm, near, load_sem.at[0]),
        pltpu.make_async_copy(density, inner.at[0:6], load_sem.at[1]),
        pltpu.make_async_copy(right_hbm, right, load_sem.at[2]),
        pltpu.make_async_copy(density, ext.at[1:7, 1:7], load_sem.at[3]),
    ]
    pl.semaphore_wait(barrier, len(peers))

    def leaf_copy(part, slot_ref, to, slot):
        return pltpu.make_async_remote_copy(
            src_ref=leaf.at[:, part], dst_ref=slot_ref.at[0], send_sem=leaf_send.at[part],
            recv_sem=leaf_recv.at[slot], device_id=to, device_id_type=MESH,
        )

    slots = (mine, other)
    for c in range(2):
        for x in range(2):
            @pl.when((core == c) & (x0 == x))
            def _(c=c, x=x):
                if c == x:
                    leaf_copy(1 - c, slots[x], (u_core, v), x).start()
                    pltpu.make_async_copy(leaf.at[:, c], slots[x].at[0], leaf_local).start()
                else:
                    leaf_copy(c, slots[x], (u, v_next), x).start()
                    leaf_copy(1 - c, slots[x], (u_core, v_next), x).start()
    for copy in loads:
        copy.start()

    up, down, west, east = u > 0, u < 7, v > 0, v < 15
    halo = [
        (density.at[0], ext.at[7, 1:7], (u - 1, v), up, down),
        (density.at[5], ext.at[0, 1:7], (u + 1, v), down, up),
    ]
    for r in range(3):
        rows = slice(2 * r, 2 * r + 2)
        to_rows = slice(2 * r + 1, 2 * r + 3)
        halo.append((density.at[rows, 0], ext.at[to_rows, 7], (u, v - 1), west, east))
        halo.append((density.at[rows, 5], ext.at[to_rows, 0], (u, v + 1), east, west))
    halo += [
        (density.at[0, 0], ext.at[7, 7], (u - 1, v - 1), up & west, down & east),
        (density.at[5, 5], ext.at[0, 0], (u + 1, v + 1), down & east, up & west),
        (density.at[0, 5], ext.at[7, 0], (u - 1, v + 1), up & east, down & west),
        (density.at[5, 0], ext.at[0, 7], (u + 1, v - 1), down & west, up & east),
    ]

    def halo_copy(n):
        source, target, to, _, _ = halo[n]
        return pltpu.make_async_remote_copy(
            src_ref=source, dst_ref=target, send_sem=halo_send.at[n], recv_sem=halo_recv.at[n],
            device_id=to, device_id_type=MESH,
        )

    def halo_start(numbers):
        for n in numbers:
            @pl.when(halo[n][3])
            def _(n=n):
                halo_copy(n).start()

    def halo_wait():
        for n in range(len(halo)):
            @pl.when(halo[n][3])
            def _(n=n):
                halo_copy(n).wait_send()

            @pl.when(halo[n][4])
            def _(n=n):
                halo_copy(n).wait_recv()

    halo_start((0, 1, 2, 3))
    zero = jnp.zeros((128, 768), jnp.bfloat16)
    ext[8, 0] = zero
    inner[6, 0] = zero
    for edge, cells in (
        (u == 0, [(0, n) for n in range(8)]),
        (u == 7, [(7, n) for n in range(8)]),
        (v == 0, [(n, 0) for n in range(8)]),
        (v == 15, [(n, 7) for n in range(8)]),
    ):
        @pl.when(edge)
        def _(cells=cells):
            for a, b in cells:
                ext[a, b] = zero
    coef[...] = jnp.zeros_like(coef)

    key = keys[...]
    rows = lax.broadcasted_iota(jnp.int32, (8, 16), 0)
    cols = lax.broadcasted_iota(jnp.int32, (8, 16), 1)
    host_row = 2 * y + x0

    def least(mask):
        return jnp.min(jnp.min(jnp.where(mask, key, 1 << 20), axis=1, keepdims=True), axis=0, keepdims=True)

    here = rows == host_row
    even = v - x0
    pairs = [(here & (cols == even), here & (cols == even + 1))]
    for bit in (2, 4, 8):
        pairs.append((here & (cols // bit == v // bit), here & (cols // bit == flip(v, bit) // bit)))
    pairs.append((here, rows == 2 * y + 1 - x0))
    for bit in (2, 4):
        pairs.append((rows // bit == u // bit, rows // bit == flip(u, bit) // bit))
    first = sketch[0:128, :]
    second = sketch[128:256, :]
    for t, (own, sibling) in enumerate(pairs):
        leads = jnp.broadcast_to((least(own) < least(sibling)).astype(f32), (128, 128)) > 0.5
        halves[t] = jnp.where(leads, first, second)
        if t == 0:
            w_mine[0] = halves[0]
            w_other[0] = jnp.where(leads, second, first)
    base[...] = dot_tn(sketch[...], sketch[...])

    def inner_pairs(low, high):
        def step(n, carry):
            j = 1 + 2 * (n % 2)
            near_pair(1 + n // 2, (j, j + 1), links, inner, 0, near, right, out, coef)
            return carry

        lax.fori_loop(low, high, step, 0)

    def edge_row(i):
        def step(n, carry):
            near_pair(i, (2 * n, 2 * n + 1), links, ext, 1, near, right, out, coef)
            return carry

        lax.fori_loop(0, 3, step, 0)

    def edge_cols(low, high):
        def step(i, carry):
            near_pair(i, (0, 5), links, ext, 1, near, right, out, coef)
            return carry

        lax.fori_loop(low, high, step, 0)

    for copy in loads:
        copy.wait()
    inner_pairs(0, 3)

    for c in range(2):
        for x in range(2):
            @pl.when((core == c) & (x0 == x))
            def _(c=c, x=x):
                if c == x:
                    pltpu.make_async_copy(leaf.at[:, c], slots[x].at[0], leaf_local).wait()
                    leaf_copy(1 - c, slots[x], (u_core, v), x).wait_send()
                    leaf_copy(0, slots[1 - x], (u_core, v), 1 - x).wait_recv()
                else:
                    for part in range(2):
                        leaf_copy(part, slots[x], (u_core, v), x).wait_send()
                    for slot in range(2):
                        leaf_copy(0, slots[slot], (u_core, v), slot).wait_recv()

    def y_copy(t, to):
        return pltpu.make_async_remote_copy(
            src_ref=mine.at[t + 1], dst_ref=other.at[t + 1], send_sem=y_send.at[t], recv_sem=y_recv.at[t],
            device_id=to, device_id_type=MESH,
        )

    def w_copy(t, to):
        return pltpu.make_async_remote_copy(
            src_ref=w_mine.at[t + 1], dst_ref=w_other.at[t + 1], send_sem=w_send.at[t], recv_sem=w_recv.at[t],
            device_id=to, device_id_type=MESH,
        )

    def cross_copy(t):
        return pltpu.make_async_remote_copy(
            src_ref=cross_send.at[t], dst_ref=cross_recv.at[t], send_sem=c_send.at[t], recv_sem=c_recv.at[t],
            device_id=(u_core, v), device_id_type=MESH,
        )

    def leaf_gram_copy(kind):
        return pltpu.make_async_remote_copy(
            src_ref=cross_send.at[LEVELS + kind], dst_ref=cross_recv.at[LEVELS + kind], send_sem=g_send.at[kind],
            recv_sem=g_recv.at[kind], device_id=(u_core, v), device_id_type=MESH,
        )

    def swap_copy():
        return pltpu.make_async_remote_copy(
            src_ref=path, dst_ref=swap, send_sem=s_send, recv_sem=s_recv,
            device_id=(u_core, v_next), device_id_type=MESH,
        )

    def row_copy(d):
        to = (v + d) % 16
        return pltpu.make_async_remote_copy(
            src_ref=term.at[to], dst_ref=from_row.at[d], send_sem=row_send.at[d], recv_sem=row_recv.at[d],
            device_id=(u, to), device_id_type=MESH,
        )

    out_copies = [
        pltpu.make_async_copy(out.at[1:5, 1:5], corrected.at[1:5, 1:5], out_sem.at[0]),
        pltpu.make_async_copy(out.at[0], corrected.at[0], out_sem.at[1]),
        pltpu.make_async_copy(out.at[5], corrected.at[5], out_sem.at[2]),
        pltpu.make_async_copy(out.at[1:5, 0], corrected.at[1:5, 0], out_sem.at[3]),
        pltpu.make_async_copy(out.at[1:5, 5], corrected.at[1:5, 5], out_sem.at[4]),
    ]

    def merge(t, carry):
        for r in range(4):
            mine[t + 1, r] = dot_nn(mine[t, r], w_mine[t]) + dot_nn(other[t, r], w_other[t])
        for step in range(LEVELS - 1):
            @pl.when(t == step)
            def _(step=step):
                y_copy(step, partners[step + 1]).start()
                if step == 1:
                    halo_start((4, 5, 8, 9))
                if step == 2:
                    halo_start((6, 7, 10, 11))

        @pl.when(t == 0)
        def _():
            merged = mine[1].reshape(512, 128)
            part = dot_tn(merged, merged)
            cross_send[LEVELS] = part
            leaf_gram_copy(0).start()
            ours = dot_tn(merged, mine[0].reshape(512, 128))
            theirs = dot_tn(merged, other[0].reshape(512, 128))
            cross_send[LEVELS + 1] = jnp.where(core == 0, theirs, ours)
            leaf_gram_copy(1).start()
            leaf_gram_copy(0).wait()
            gram[...] = part + cross_recv[LEVELS]
            leaf_gram_copy(1).wait()
            path[...] = jnp.where(core == 0, ours, theirs) + cross_recv[LEVELS + 1]

        @pl.when(t > 0)
        def _():
            mixed = dot_nn(cross[...], w_other[t])
            half = dot_tn(w_mine[t], mixed)
            gram[...] = base[...] + half + half.T
            path[...] = dot_tn(halves[t], path[...]) + dot_tn(mixed, dot_tn(linv[...], path[...]))

        cholesky_inverse(gram, linv)

        @pl.when(t < LEVELS - 1)
        def _():
            w_mine[t + 1] = dot_tn(linv[...], halves[t + 1])

        for step in range(LEVELS - 1):
            @pl.when(t == step)
            def _(step=step):
                w_copy(step, partners[step + 1]).start()

        path[...] = dot_nn(linv[...], path[...])

        @pl.when((t == 4) & (core != x0))
        def _():
            swap_copy().start()
            swap_copy().wait()
            path[...] = swap[...]

        @pl.when(t == 0)
        def _():
            inner_pairs(3, 8)
            out_copies[0].start()

        @pl.when(t == 3)
        def _():
            halo_wait()
            edge_row(0)
            out_copies[1].start()

        @pl.when(t == 4)
        def _():
            edge_row(5)
            out_copies[2].start()

        @pl.when(t == 5)
        def _():
            edge_cols(1, 5)
            out_copies[3].start()
            out_copies[4].start()
            products = lax.dot_general(
                coef[...], path[...], (((0,), (1,)), ((), ())), precision=highest, preferred_element_type=f32
            )
            term[...] = products.reshape(16, 48, 128)
            for d in range(1, 16):
                row_copy(d).start()
            path[...] = diag_matrix()

        @pl.when(t < LEVELS - 1)
        def _():
            y_copy(t, (u_core, v)).wait()
            part = dot_tn(mine[t + 1].reshape(512, 128), other[t + 1].reshape(512, 128))
            cross_send[t] = part
            cross_copy(t).start()
            cross_copy(t).wait()
            cross[...] = part + cross_recv[t]
            w_copy(t, (u_core, v)).wait()

        return carry

    def diag_matrix():
        down_iota = lax.broadcasted_iota(jnp.int32, (128, 128), 0)
        return jnp.where(down_iota == lax.broadcasted_iota(jnp.int32, (128, 128), 1), 1.0, 0.0).astype(f32)

    lax.fori_loop(0, LEVELS, merge, 0)
    total = term[v]
    for d in range(1, 16):
        row_copy(d).wait()
        total = total + from_row[d]
    total = dot_nt(total, path[...])
    row_sum[...] = total
    copies = []
    for d in range(1, 8):
        copy = pltpu.make_async_remote_copy(
            src_ref=row_sum, dst_ref=from_col.at[d], send_sem=col_send.at[d], recv_sem=col_recv.at[d],
            device_id=((u + d) % 8, v), device_id_type=MESH,
        )
        copy.start()
        copies.append(copy)
    root = dot_nt(mine[LEVELS, y], linv[...])
    for copy in out_copies:
        copy.wait()
    for d in range(1, 8):
        copies[d - 1].wait()
        total = total + from_col[d]
    far_out[...] = dot_nt(root, total)


def solve(links, density, near_blocks, far_right, far_left, sketch, keys):
    anywhere = pl.BlockSpec(memory_space=pl.ANY)
    vmem = pl.BlockSpec(memory_space=pltpu.VMEM)
    dma = pltpu.SemaphoreType.DMA
    bf16 = jnp.bfloat16
    return pl.pallas_call(
        solver_kernel,
        out_shape=(jax.ShapeDtypeStruct((6, 6, 128, 768), bf16), jax.ShapeDtypeStruct((128, 48), f32)),
        in_specs=[pl.BlockSpec(memory_space=pltpu.SMEM)] + [anywhere] * 4 + [vmem, vmem],
        out_specs=(anywhere, vmem),
        scratch_shapes=[
            pltpu.VMEM((9, 8, 128, 768), bf16),
            pltpu.VMEM((7, 6, 128, 768), bf16),
            pltpu.VMEM((6, 6, 6, 128, 128), bf16),
            pltpu.VMEM((6, 6, 128, 128), bf16),
            pltpu.VMEM((6, 6, 128, 768), bf16),
            pltpu.VMEM((128, 768), f32),
            pltpu.VMEM((LEVELS + 1, 4, 128, 128), f32),
            pltpu.VMEM((LEVELS + 1, 4, 128, 128), f32),
            pltpu.VMEM((LEVELS + 1, 128, 128), f32),
            pltpu.VMEM((LEVELS + 1, 128, 128), f32),
            pltpu.VMEM((LEVELS, 128, 128), f32),
            pltpu.VMEM((128, 128), f32),
            pltpu.VMEM((LEVELS + 2, 128, 128), f32),
            pltpu.VMEM((LEVELS + 2, 128, 128), f32),
            pltpu.VMEM((128, 128), f32),
            pltpu.VMEM((128, 128), f32),
            pltpu.VMEM((128, 128), f32),
            pltpu.VMEM((128, 128), f32),
            pltpu.VMEM((128, 128), f32),
            pltpu.VMEM((16, 48, 128), f32),
            pltpu.VMEM((16, 48, 128), f32),
            pltpu.VMEM((48, 128), f32),
            pltpu.VMEM((8, 48, 128), f32),
            dma((4,)), dma((5,)), dma((12,)), dma((12,)),
            dma, dma((2,)), dma((2,)),
            dma((LEVELS,)), dma((LEVELS,)), dma((LEVELS,)), dma((LEVELS,)),
            dma((LEVELS,)), dma((LEVELS,)), dma((2,)), dma((2,)), dma, dma,
            dma((16,)), dma((16,)), dma((8,)), dma((8,)),
        ],
        compiler_params=pltpu.CompilerParams(collective_id=0, has_side_effects=True, vmem_limit_bytes=60 * 2**20),
        cost_estimate=pl.CostEstimate(flops=10**10, bytes_accessed=2**25, transcendentals=0),
        name="solver",
    )(links.reshape(6, 36), density, near_blocks, far_right, far_left.reshape(4, 2, 128, 128), sketch, keys)


def copy_kernel(source, target, held, in_sem, out_sem):
    reads = [pltpu.make_async_copy(source.at[i], held.at[i], in_sem.at[i]) for i in range(6)]
    writes = [pltpu.make_async_copy(held.at[i], target.at[i], out_sem.at[i]) for i in range(6)]
    for copy in reads:
        copy.start()
    for read, write in zip(reads, writes):
        read.wait()
        write.start()
    for copy in writes:
        copy.wait()


def copied(value):
    anywhere = pl.BlockSpec(memory_space=pl.ANY)
    return pl.pallas_call(
        copy_kernel,
        out_shape=jax.ShapeDtypeStruct(value.shape, value.dtype),
        in_specs=[anywhere],
        out_specs=anywhere,
        scratch_shapes=[
            pltpu.VMEM(value.shape, value.dtype), pltpu.SemaphoreType.DMA((6,)), pltpu.SemaphoreType.DMA((6,)),
        ],
        compiler_params=pltpu.CompilerParams(vmem_limit_bytes=16 * 2**20),
        name="copy_out",
    )(value)


def per_device(density, near_blocks, neighbours, far_right, far_left, sketch, patch_order):
    corrected, far_field = solve(
        neighbours, density, near_blocks, far_right, far_left, sketch, patch_order.reshape(8, 16)
    )
    return (copied(corrected), far_field)


def solution(mesh):
    in_specs = (
        P("pu", "pv", None, None),
        P("pu", "pv", None, None, None),
        P("pu", "pv", None),
        P("pu", "pv", None, None),
        P("pu", "pv", None, None),
        P(),
        P(),
    )
    out_specs = (P("pu", "pv", None, None), P("pu", "pv"))
    return jax.shard_map(
        per_device, mesh=mesh, in_specs=in_specs, out_specs=out_specs, check_vma=False
    )
```

time: 192 us -> 139 us (0.72)
  Pallas kernels: 158 us -> 131 us
  waiting for transfers between devices: 13.1 us -> 0 us
  starting transfers between devices: 12.9 us -> 0 us
    pallas_call x3 -> x2, Pallas kernels: 158 us -> 131 us  [the longest x1 127 us: solve(): pl.pallas_call(solver_kernel, out_shape=(jax.ShapeDtypeStruct((6, 6, 128,...]
    ppermute x4 -> x0, waiting for transfers between devices: 13.1 us -> none  [the longest x2 12.3 us: from_sides(): high = lax.ppermute(lax.slice_in_dim(block, 0, 1, axis=dim), axis, backward)]
    ppermute x4 -> x0, starting transfers between devices: 12.9 us -> none  [the longest x2 8.33 us: from_sides(): lax.ppermute(lax.slice_in_dim(block, block.shape[dim] - 1, None, axis=dim...]
    reshape x2, local copies, waits for them, and re-layouts: 0.15 us -> 2.73 us  [the longest x1 1.4 us: solve(): links.reshape(6, 36)]
    slice x3 -> x0, local copies, waits for them, and re-layouts: 1.95 us -> none  [the longest x1 1.9 us: from_sides(): high = lax.ppermute(lax.slice_in_dim(block, 0, 1, axis=dim), axis, backward)]
  transfers between devices with their start and end apart: 4 -> 0, of which waited for: 2 -> 0; matrix products, arithmetic and copies ran while one was open for 0% -> 0% of each run, Pallas kernels for 64% -> 0%
where the time goes in v2:
time: 139 us; the launch traced here: 138 us
  Pallas kernels  131 us (94%)
  local copies, waits for them, and re-layouts  6.42 us (5%)
    pallas_call x1, Pallas kernels, solve(): pl.pallas_call(solver_kernel, out_shape=(jax.ShapeDtypeStruct((6, 6, 128,...  127 us
    pallas_call x1, Pallas kernels, copied(): pl.pallas_call(copy_kernel, out_shape=jax.ShapeDtypeStruct(value.shape, v...  4.46 us
    unnamed x5, local copies, waits for them, and re-layouts  3.69 us

profile of v2, /device:TPU:1, one launch (start us, length us, event | category | flops | bytes accessed | tf_op | source)
XLA Modules:
  0.0 138.4 jit_solution(11396155765137338486)
XLA Ops:
  0.6 1.4 %reshape.13.links = s32[6,36]{1,0:T(8,128)} reshape(s32[6,6,6]{2,1,0:T(8,128)} %param.9) | data formatting | bytes 1728 | tf_op jit(solution)/shard_map/reshape | solution.py:507
  2.0 1.3 reshape.15.keys
  3.4 126.9 %solver.1 = (bf16[6,6,128,768]{3,2,1,0:T(8,128)(2,1)}, f32[128,48]{1,0:T(8,128)}) custom-call(s32[6,36]{1,0:T(8,128)} %reshape.13.links, bf16[6,6,128,768]{3,2,1,0:T(8,128)(2,1)} %density.1, bf16[6,6,6,128,128]{4,3,2,1,0:T(8,128)(2,1)} %near_hbm.1, bf16[6,6,128,128]{3,2,1,0:T(8,128)(2,1)} %right_hbm.1, f32[4,2,128,128]{3,2,1,0:T(8,128)} %bitcast.1, ...), custom_call_target="tpu_custom_call" | custom-call | flops 10000000000 | bytes 33554432 | tf_op jit(solution)/shard_map/solver/pallas_call | solution.py:469
  130.2 0.0 copy-start
  130.2 3.0 %copy-done = bf16[6,6,128,768]{3,2,1,0:T(8,128)(2,1)S(1)} copy-done((bf16[6,6,128,768]{3,2,1,0:T(8,128)(2,1)S(1)}, bf16[6,6,128,768]{3,2,1,0:T(8,128)(2,1)}, u32[]{:S(2)}) %copy-start) | copy-done | bytes 7077912
  133.2 0.0 copy-start.1
  133.3 4.5 %copy_out.1 = bf16[6,6,128,768]{3,2,1,0:T(8,128)(2,1)} custom-call(bf16[6,6,128,768]{3,2,1,0:T(8,128)(2,1)S(1)} %copy-done), custom_call_target="tpu_custom_call" | custom-call | tf_op jit(solution)/shard_map/copy_out/pallas_call | solution.py:524
  137.7 0.0 copy-done.1
  137.7 0.7 copy.9
Async XLA Ops:
  130.2 3.0 %copy-start = (bf16[6,6,128,768]{3,2,1,0:T(8,128)(2,1)S(1)}, bf16[6,6,128,768]{3,2,1,0:T(8,128)(2,1)}, u32[]{:S(2)}) copy-start(bf16[6,6,128,768]{3,2,1,0:T(8,128)(2,1)} %get-tuple-element.4.source) | copy-start | bytes 21233668
  133.2 4.5 %copy-start.1 = (f32[128,48]{1,0:T(8,128)S(1)}, f32[128,48]{1,0:T(8,128)}, u32[]{:S(2)}) copy-start(f32[128,48]{1,0:T(8,128)} %get-tuple-element.7) | copy-start | bytes 73732

commit v3 on v2

v3 whole, which is shorter than its diff:
```python
import functools

import jax
import jax.numpy as jnp
from jax import lax
from jax.experimental import pallas as pl
from jax.experimental.pallas import tpu as pltpu
from jax.sharding import PartitionSpec as P

MESH = pl.DeviceIdType.MESH
highest = lax.Precision.HIGHEST
f32 = jnp.float32
LEVELS = 7
INNER = (0, 3, 6, 9, 12)


def dot_nn(a, b):
    return lax.dot_general(a, b, (((1,), (0,)), ((), ())), precision=highest, preferred_element_type=f32)


def dot_tn(a, b):
    return lax.dot_general(a, b, (((0,), (0,)), ((), ())), precision=highest, preferred_element_type=f32)


def dot_nt(a, b):
    return lax.dot_general(a, b, (((1,), (1,)), ((), ())), precision=highest, preferred_element_type=f32)


def tile(x):
    return jnp.broadcast_to(x, (8, 128))


def tree_sum(terms):
    while len(terms) > 1:
        terms = [terms[i] + terms[i + 1] if i + 1 < len(terms) else terms[i] for i in range(0, len(terms), 2)]
    return terms[0]


def cholesky_inverse(gram, out_ref, panels):
    groups = 16
    row = lax.broadcasted_iota(jnp.int32, (8, 128), 0)
    lane = lax.broadcasted_iota(jnp.int32, (8, 128), 1)
    left = [gram[8 * g : 8 * g + 8, :] for g in range(groups)]
    right = [jnp.where(lane == row + 8 * g, 1.0, 0.0).astype(f32) for g in range(groups)]
    for b in range(groups):
        base = 8 * b
        last = b == groups - 1
        cols = [[tile(left[g][:, base + k : base + k + 1]) for k in range(8)] for g in range(b, groups)]
        for k in range(8):
            panels[b, k] = cols[0][k]
        panels[b, 8] = left[b]
        panels[b, 9] = right[b]
        d = [[tile(panels[b, k, i : i + 1, :]) for k in range(i + 1)] for i in range(8)]
        low = [[None] * 8 for _ in range(8)]
        inv = [[None] * 8 for _ in range(8)]
        for k in range(0, 8, 2):
            p, q, r = d[k][k], d[k + 1][k], d[k + 1][k + 1]
            scale = lax.rsqrt(p)
            second = lax.rsqrt(p * r - q * q)
            both = scale * second
            low[k + 1][k] = q * scale
            for i in range(k + 2, 8):
                low[i][k] = d[i][k] * scale
                low[i][k + 1] = (p * d[i][k + 1] - d[i][k] * q) * both
            for m in range(k + 2, 8):
                for i in range(m, 8):
                    d[i][m] = d[i][m] - (low[i][k] * low[m][k] + low[i][k + 1] * low[m][k + 1])
            for n, pivot in ((k, scale), (k + 1, p * both)):
                inv[n][n] = pivot
                for j in range(n):
                    inv[n][j] = -(pivot * tree_sum([low[n][h] * inv[h][j] for h in range(j, n)]))

        def solved(panel):
            return [tree_sum([inv[i][k] * panel[k] for k in range(i + 1)]) for i in range(8)]

        def solved_again(up):
            return [tree_sum([inv[i][k] * up[i] for i in range(k, 8)]) for k in range(8)]

        up_right = solved([tile(panels[b, 9, k : k + 1, :]) for k in range(8)])
        for i in range(8):
            out_ref[base + i : base + i + 1, :] = up_right[i][0:1, :]
        if last:
            break
        full_left = solved_again(solved([tile(panels[b, 8, k : k + 1, :]) for k in range(8)]))
        full_right = solved_again(up_right)
        for g in range(b + 1, groups):
            c = cols[g - b]
            left[g] = left[g] - tree_sum([c[k] * full_left[k] for k in range(8)])
            right[g] = right[g] - tree_sum([c[k] * full_right[k] for k in range(8)])


def flip(index, bit):
    return index + bit - 2 * bit * ((index // bit) % 2)


def near_pair(i, cols, places, links, source, near, right, out, coef):
    done = []
    for j, place in zip(cols, places):
        where = []
        for s in range(6):
            e = links[i, j, s]
            down = (e * 11) // 32
            across = e - 3 * down
            where.append((jnp.where(e < 9, i + down, 8), jnp.where(e < 9, place + across - 1, 0)))
        lhs = jnp.concatenate([near[i, j, s] for s in range(6)], axis=1)
        rhs = jnp.concatenate([source[a, b] for a, b in where], axis=0)
        summed = jnp.dot(lhs, rhs, preferred_element_type=f32)
        block = (source[i + 1, place].astype(f32) + summed).astype(jnp.bfloat16)
        out[i, j] = block
        done.append(block)
    lhs = jnp.concatenate([right[i, j] for j in cols], axis=0)
    coef[...] += lax.dot_general(
        lhs, jnp.concatenate(done, axis=0), (((0,), (0,)), ((), ())), preferred_element_type=f32
    )


def split(value):
    high = value.astype(jnp.bfloat16)
    return high, (value - high.astype(f32)).astype(jnp.bfloat16)


def dot_sum(a, b, wide):
    a_high, a_low = split(a)
    b_high, b_low = split(b)
    return jnp.dot(
        jnp.concatenate([a_high, b_high, a_high, b_high, a_low, b_low], axis=1), wide, preferred_element_type=f32
    )


def widened(a, b):
    a_high, a_low = split(a)
    b_high, b_low = split(b)
    return jnp.concatenate([a_high, b_high, a_low, b_low, a_high, b_high], axis=0)


def solver_kernel(
    links, density, near_hbm, right_hbm, leaf, sketch, keys, corrected, far_out,
    ext, inner, near, right, out, coef,
    mine, other, w_mine, w_other, halves, base, cross_send, cross_recv, cross, gram, mixed, panels, linv, path, swap,
    term, from_row, row_sum, from_col,
    load_sem, out_sem, halo_send, halo_recv,
    leaf_local, leaf_send, leaf_recv, y_send, y_recv, w_send, w_recv, c_send, c_recv, g_send, g_recv, s_send, s_recv,
    row_send, row_recv, col_send, col_recv,
):
    u = lax.axis_index("pu")
    v = lax.axis_index("pv")
    core = u % 2
    y = u // 2
    x0 = v % 2
    u_core = flip(u, 1)
    v_next = flip(v, 1)
    partners = {1: (u, flip(v, 2)), 2: (u, flip(v, 4)), 3: (u, flip(v, 8)), 4: (u, v_next), 5: (flip(u, 2), v), 6: (flip(u, 4), v)}
    barrier = pltpu.get_barrier_semaphore()
    peers = list(partners.values()) + [(u_core, v), (u_core, v_next)]
    for du in (7, 0, 1):
        for dv in (15, 0, 1):
            if du or dv:
                peers.append(((u + du) % 8, (v + dv) % 16))
    for peer in peers:
        pl.semaphore_signal(barrier, inc=1, device_id=peer, device_id_type=MESH)
    loads = [
        pltpu.make_async_copy(near_hbm, near, load_sem.at[0]),
        pltpu.make_async_copy(density, inner.at[1:7], load_sem.at[1]),
        pltpu.make_async_copy(right_hbm, right, load_sem.at[2]),
        pltpu.make_async_copy(density.at[:, 0:2], ext.at[1:7, 1:3], load_sem.at[3]),
        pltpu.make_async_copy(density.at[:, 4:6], ext.at[1:7, 3:5], load_sem.at[4]),
    ]
    for copy in loads:
        copy.start()
    key = keys[...]
    patch = lax.broadcasted_iota(jnp.int32, (1, 128), 1)
    rows = patch // 16
    cols = patch % 16
    host_row = 2 * y + x0

    def least(mask):
        return jnp.min(jnp.where(mask, key, 1 << 20), axis=1, keepdims=True)

    here = rows == host_row
    even = v - x0
    pairs = [(here & (cols == even), here & (cols == even + 1))]
    for bit in (2, 4, 8):
        pairs.append((here & (cols // bit == v // bit), here & (cols // bit == flip(v, bit) // bit)))
    pairs.append((here, rows == 2 * y + 1 - x0))
    for bit in (2, 4):
        pairs.append((rows // bit == u // bit, rows // bit == flip(u, bit) // bit))
    first = sketch[0:128, :]
    second = sketch[128:256, :]
    for t, (own, sibling) in enumerate(pairs):
        leads = jnp.broadcast_to((least(own) < least(sibling)).astype(f32), (128, 128)) > 0.5
        halves[t] = jnp.where(leads, first, second)
        if t == 0:
            w_mine[0] = halves[0]
            w_other[0] = jnp.where(leads, second, first)
    base[...] = dot_tn(sketch[...], sketch[...])
    pl.semaphore_wait(barrier, len(peers))

    def leaf_copy(part, slot_ref, to, slot):
        return pltpu.make_async_remote_copy(
            src_ref=leaf.at[:, part], dst_ref=slot_ref.at[0], send_sem=leaf_send.at[part],
            recv_sem=leaf_recv.at[slot], device_id=to, device_id_type=MESH,
        )

    slots = (mine, other)
    for c in range(2):
        for x in range(2):
            @pl.when((core == c) & (x0 == x))
            def _(c=c, x=x):
                if c == x:
                    leaf_copy(1 - c, slots[x], (u_core, v), x).start()
                    pltpu.make_async_copy(leaf.at[:, c], slots[x].at[0], leaf_local).start()
                else:
                    leaf_copy(c, slots[x], (u, v_next), x).start()
                    leaf_copy(1 - c, slots[x], (u_core, v_next), x).start()
    up, down, west, east = u > 0, u < 7, v > 0, v < 15
    turn_west, turn_east = v % 4 == 0, v % 4 == 3
    halo = [
        (density.at[0], inner.at[7], (u - 1, v), up, down, None),
        (density.at[5], inner.at[0], (u + 1, v), down, up, None),
    ]
    for r in range(3):
        span = slice(2 * r, 2 * r + 2)
        to_span = slice(2 * r + 1, 2 * r + 3)
        halo.append((density.at[span, 0], ext.at[to_span, 5], (u, v - 1), west, east, turn_west))
        halo.append((density.at[span, 5], ext.at[to_span, 0], (u, v + 1), east, west, turn_east))
    halo += [
        (density.at[0, 0], ext.at[7, 5], (u - 1, v - 1), up & west, down & east, turn_west),
        (density.at[5, 5], ext.at[0, 0], (u + 1, v + 1), down & east, up & west, turn_east),
        (density.at[0, 5], ext.at[7, 0], (u - 1, v + 1), up & east, down & west, turn_east),
        (density.at[5, 0], ext.at[0, 5], (u + 1, v - 1), down & west, up & east, turn_west),
    ]

    def halo_copy(n):
        source, target, to = halo[n][:3]
        return pltpu.make_async_remote_copy(
            src_ref=source, dst_ref=target, send_sem=halo_send.at[n], recv_sem=halo_recv.at[n],
            device_id=to, device_id_type=MESH,
        )

    def halo_start(numbers, only=None):
        for n in numbers:
            due = halo[n][3]
            if only is not None:
                due = due & only

            @pl.when(due)
            def _(n=n):
                halo_copy(n).start()

    def halo_wait(numbers):
        for n in numbers:
            @pl.when(halo[n][3])
            def _(n=n):
                halo_copy(n).wait_send()

            @pl.when(halo[n][4])
            def _(n=n):
                halo_copy(n).wait_recv()

    even_v, odd_v = x0 == 0, x0 == 1
    halo_start((0, 1))
    halo_start((2,), even_v)
    halo_start((3,), odd_v)
    halo_start((4,), turn_west)
    halo_start((5,), turn_east)
    zero = jnp.zeros((128, 768), jnp.bfloat16)
    ext[8, 0] = zero
    inner[8, 0] = zero
    for edge, target, cells in (
        (u == 0, inner, [(0, n) for n in range(6)]),
        (u == 7, inner, [(7, n) for n in range(6)]),
        (u == 0, ext, [(0, 0), (0, 5)]),
        (u == 7, ext, [(7, 0), (7, 5)]),
        (v == 0, ext, [(n, 0) for n in range(8)]),
        (v == 15, ext, [(n, 5) for n in range(8)]),
    ):
        @pl.when(edge)
        def _(target=target, cells=cells):
            for a, b in cells:
                target[a, b] = zero
    coef[...] = jnp.zeros_like(coef)

    def inner_pairs(low, high):
        def step(n, carry):
            j = 1 + 2 * (n % 2)
            near_pair(n // 2, (j, j + 1), (j, j + 1), links, inner, near, right, out, coef)
            return carry

        lax.fori_loop(low, high, step, 0)

    def side_pairs(low, high):
        def step(i, carry):
            near_pair(i, (0, 5), (1, 4), links, ext, near, right, out, coef)
            return carry

        lax.fori_loop(low, high, step, 0)

    for c in range(2):
        for x in range(2):
            @pl.when((core == c) & (x0 == x))
            def _(c=c, x=x):
                if c == x:
                    pltpu.make_async_copy(leaf.at[:, c], slots[x].at[0], leaf_local).wait()
                    leaf_copy(1 - c, slots[x], (u_core, v), x).wait_send()
                    leaf_copy(0, slots[1 - x], (u_core, v), 1 - x).wait_recv()
                else:
                    for part in range(2):
                        leaf_copy(part, slots[x], (u_core, v), x).wait_send()
                    for slot in range(2):
                        leaf_copy(0, slots[slot], (u_core, v), slot).wait_recv()

    halo_start((2,), odd_v)
    halo_start((3,), even_v)
    straight_west, straight_east = jnp.logical_not(turn_west), jnp.logical_not(turn_east)

    def y_copy(t, part, to):
        span = slice(2 * part, 2 * part + 2)
        return pltpu.make_async_remote_copy(
            src_ref=mine.at[t + 1, span], dst_ref=other.at[t + 1, span],
            send_sem=y_send.at[t, part], recv_sem=y_recv.at[t, part],
            device_id=to, device_id_type=MESH,
        )

    def w_copy(t, to):
        return pltpu.make_async_remote_copy(
            src_ref=w_mine.at[t + 1], dst_ref=w_other.at[t + 1], send_sem=w_send.at[t], recv_sem=w_recv.at[t],
            device_id=to, device_id_type=MESH,
        )

    def cross_copy(t):
        return pltpu.make_async_remote_copy(
            src_ref=cross_send.at[t], dst_ref=cross_recv.at[t], send_sem=c_send.at[t], recv_sem=c_recv.at[t],
            device_id=(u_core, v), device_id_type=MESH,
        )

    def leaf_gram_copy(kind):
        return pltpu.make_async_remote_copy(
            src_ref=cross_send.at[LEVELS + kind], dst_ref=cross_recv.at[LEVELS + kind], send_sem=g_send.at[kind],
            recv_sem=g_recv.at[kind], device_id=(u_core, v), device_id_type=MESH,
        )

    def swap_copy():
        return pltpu.make_async_remote_copy(
            src_ref=path, dst_ref=swap, send_sem=s_send, recv_sem=s_recv,
            device_id=(u_core, v_next), device_id_type=MESH,
        )

    def row_copy(d):
        to = (v + d) % 16
        return pltpu.make_async_remote_copy(
            src_ref=term.at[to], dst_ref=from_row.at[d], send_sem=row_send.at[d], recv_sem=row_recv.at[d],
            device_id=(u, to), device_id_type=MESH,
        )

    out_copies = [
        pltpu.make_async_copy(out.at[:, 1:5], corrected.at[:, 1:5], out_sem.at[0]),
        pltpu.make_async_copy(out.at[:, 0], corrected.at[:, 0], out_sem.at[1]),
        pltpu.make_async_copy(out.at[:, 5], corrected.at[:, 5], out_sem.at[2]),
    ]

    def merge(t, carry):
        wide = widened(w_mine[t], w_other[t])
        for part in range(2):
            span = slice(2 * part, 2 * part + 2)
            both = dot_sum(mine[t, span].reshape(256, 128), other[t, span].reshape(256, 128), wide)
            mine[t + 1, span] = both.reshape(2, 128, 128)
            for step in range(LEVELS - 1):
                @pl.when(t == step)
                def _(step=step, part=part):
                    y_copy(step, part, partners[step + 1]).start()

        @pl.when(t == 1)
        def _():
            halo_start((4, 8), straight_west)
            halo_start((5, 9), straight_east)

        @pl.when(t == 2)
        def _():
            halo_start((6, 11), straight_west)
            halo_start((7, 10), straight_east)

        @pl.when(t == 3)
        def _():
            halo_start((6, 8, 11), turn_west)
            halo_start((7, 9, 10), turn_east)

        @pl.when(t == 0)
        def _():
            merged = mine[1].reshape(512, 128)
            part = dot_tn(merged, merged)
            cross_send[LEVELS] = part
            leaf_gram_copy(0).start()
            ours = dot_tn(merged, mine[0].reshape(512, 128))
            theirs = dot_tn(merged, other[0].reshape(512, 128))
            cross_send[LEVELS + 1] = jnp.where(core == 0, theirs, ours)
            leaf_gram_copy(1).start()
            leaf_gram_copy(0).wait()
            gram[...] = part + cross_recv[LEVELS]
            leaf_gram_copy(1).wait()
            path[...] = jnp.where(core == 0, ours, theirs) + cross_recv[LEVELS + 1]

        @pl.when(t > 0)
        def _():
            mixed[...] = dot_nn(cross[...], w_other[t])
            half = dot_tn(w_mine[t], mixed[...])
            gram[...] = base[...] + half + half.T

        cholesky_inverse(gram, linv.at[t], panels)

        @pl.when(t < LEVELS - 1)
        def _():
            w_mine[t + 1] = dot_tn(linv[t], halves[t + 1])

        for step in range(LEVELS - 1):
            @pl.when(t == step)
            def _(step=step):
                w_copy(step, partners[step + 1]).start()

        @pl.when(t < LEVELS - 1)
        def _():
            y_copy(t, 0, (u_core, v)).wait()
            part = dot_tn(mine[t + 1, 0:2].reshape(256, 128), other[t + 1, 0:2].reshape(256, 128))
            y_copy(t, 1, (u_core, v)).wait()
            part = part + dot_tn(mine[t + 1, 2:4].reshape(256, 128), other[t + 1, 2:4].reshape(256, 128))
            cross_send[t] = part
            cross_copy(t).start()

        @pl.when(t > 0)
        def _():
            path[...] = dot_tn(halves[t], path[...]) + dot_tn(mixed[...], dot_tn(linv[t - 1], path[...]))

        path[...] = dot_nn(linv[t], path[...])

        @pl.when((t == 4) & (core != x0))
        def _():
            swap_copy().start()

        @pl.when(t == 0)
        def _():
            for copy in loads:
                copy.wait()
            halo_wait((0, 1))
            for a in (0, 7):
                for place, col in ((1, 0), (2, 1), (3, 4), (4, 5)):
                    ext[a, place] = inner[a, col]

        for step in range(4):
            @pl.when(t == step)
            def _(step=step):
                inner_pairs(INNER[step], INNER[step + 1])

        @pl.when(t == 4)
        def _():
            out_copies[0].start()
            halo_wait(range(2, 12))
            side_pairs(0, 3)

        @pl.when((t == 4) & (core != x0))
        def _():
            swap_copy().wait()
            path[...] = swap[...]

        @pl.when(t == 5)
        def _():
            side_pairs(3, 6)
            out_copies[1].start()
            out_copies[2].start()
            products = lax.dot_general(
                coef[...], path[...], (((0,), (1,)), ((), ())), precision=highest, preferred_element_type=f32
            )
            term[...] = products.reshape(16, 48, 128)
            for d in range(1, 16):
                row_copy(d).start()
            path[...] = diag_matrix()

        @pl.when(t < LEVELS - 1)
        def _():
            cross_copy(t).wait()
            cross[...] = cross_send[t] + cross_recv[t]
            w_copy(t, (u_core, v)).wait()

        return carry

    def diag_matrix():
        down_iota = lax.broadcasted_iota(jnp.int32, (128, 128), 0)
        return jnp.where(down_iota == lax.broadcasted_iota(jnp.int32, (128, 128), 1), 1.0, 0.0).astype(f32)

    lax.fori_loop(0, LEVELS, merge, 0)
    total = term[v]
    for d in range(1, 16):
        row_copy(d).wait()
        total = total + from_row[d]
    total = dot_nt(total, path[...])
    row_sum[...] = total
    copies = []
    for d in range(1, 8):
        copy = pltpu.make_async_remote_copy(
            src_ref=row_sum, dst_ref=from_col.at[d], send_sem=col_send.at[d], recv_sem=col_recv.at[d],
            device_id=((u + d) % 8, v), device_id_type=MESH,
        )
        copy.start()
        copies.append(copy)
    root = dot_nt(mine[LEVELS, y], linv[LEVELS - 1])
    for copy in out_copies:
        copy.wait()
    for d in range(1, 8):
        copies[d - 1].wait()
        total = total + from_col[d]
    far_out[...] = dot_nt(root, total)


def solve(links, density, near_blocks, far_right, far_left, sketch, keys):
    anywhere = pl.BlockSpec(memory_space=pl.ANY)
    vmem = pl.BlockSpec(memory_space=pltpu.VMEM)
    dma = pltpu.SemaphoreType.DMA
    bf16 = jnp.bfloat16
    return pl.pallas_call(
        solver_kernel,
        out_shape=(jax.ShapeDtypeStruct((6, 6, 128, 768), bf16), jax.ShapeDtypeStruct((128, 48), f32)),
        in_specs=[pl.BlockSpec(memory_space=pltpu.SMEM)] + [anywhere] * 4 + [vmem, vmem],
        out_specs=(anywhere, vmem),
        scratch_shapes=[
            pltpu.VMEM((9, 6, 128, 768), bf16),
            pltpu.VMEM((9, 6, 128, 768), bf16),
            pltpu.VMEM((6, 6, 6, 128, 128), bf16),
            pltpu.VMEM((6, 6, 128, 128), bf16),
            pltpu.VMEM((6, 6, 128, 768), bf16),
            pltpu.VMEM((128, 768), f32),
            pltpu.VMEM((LEVELS + 1, 4, 128, 128), f32),
            pltpu.VMEM((LEVELS + 1, 4, 128, 128), f32),
            pltpu.VMEM((LEVELS + 1, 128, 128), f32),
            pltpu.VMEM((LEVELS + 1, 128, 128), f32),
            pltpu.VMEM((LEVELS, 128, 128), f32),
            pltpu.VMEM((128, 128), f32),
            pltpu.VMEM((LEVELS + 2, 128, 128), f32),
            pltpu.VMEM((LEVELS + 2, 128, 128), f32),
            pltpu.VMEM((128, 128), f32),
            pltpu.VMEM((128, 128), f32),
            pltpu.VMEM((128, 128), f32),
            pltpu.VMEM((16, 10, 8, 128), f32),
            pltpu.VMEM((LEVELS, 128, 128), f32),
            pltpu.VMEM((128, 128), f32),
            pltpu.VMEM((128, 128), f32),
            pltpu.VMEM((16, 48, 128), f32),
            pltpu.VMEM((16, 48, 128), f32),
            pltpu.VMEM((48, 128), f32),
            pltpu.VMEM((8, 48, 128), f32),
            dma((5,)), dma((3,)), dma((12,)), dma((12,)),
            dma, dma((2,)), dma((2,)),
            dma((LEVELS, 2)), dma((LEVELS, 2)), dma((LEVELS,)), dma((LEVELS,)),
            dma((LEVELS,)), dma((LEVELS,)), dma((2,)), dma((2,)), dma, dma,
            dma((16,)), dma((16,)), dma((8,)), dma((8,)),
        ],
        compiler_params=pltpu.CompilerParams(collective_id=0, has_side_effects=True, vmem_limit_bytes=60 * 2**20),
        cost_estimate=pl.CostEstimate(flops=10**10, bytes_accessed=2**25, transcendentals=0),
        name="solver",
    )(links, density, near_blocks, far_right, far_left.reshape(4, 2, 128, 128), sketch, keys)


def copy_kernel(source, target, held, in_sem, out_sem):
    reads = [pltpu.make_async_copy(source.at[i], held.at[i], in_sem.at[i]) for i in range(6)]
    writes = [pltpu.make_async_copy(held.at[i], target.at[i], out_sem.at[i]) for i in range(6)]
    for copy in reads:
        copy.start()
    for read, write in zip(reads, writes):
        read.wait()
        write.start()
    for copy in writes:
        copy.wait()


def copied(value):
    anywhere = pl.BlockSpec(memory_space=pl.ANY)
    return pl.pallas_call(
        copy_kernel,
        out_shape=jax.ShapeDtypeStruct(value.shape, value.dtype),
        in_specs=[anywhere],
        out_specs=anywhere,
        scratch_shapes=[
            pltpu.VMEM(value.shape, value.dtype), pltpu.SemaphoreType.DMA((6,)), pltpu.SemaphoreType.DMA((6,)),
        ],
        compiler_params=pltpu.CompilerParams(vmem_limit_bytes=60 * 2**20),
        name="copy_out",
    )(value)


def per_device(density, near_blocks, neighbours, far_right, far_left, sketch, patch_order):
    corrected, far_field = solve(
        neighbours, density, near_blocks, far_right, far_left, sketch, patch_order.reshape(1, 128)
    )
    return (copied(corrected), far_field)


def solution(mesh):
    in_specs = (
        P("pu", "pv", None, None),
        P("pu", "pv", None, None, None),
        P("pu", "pv", None),
        P("pu", "pv", None, None),
        P("pu", "pv", None, None),
        P(),
        P(),
    )
    out_specs = (P("pu", "pv", None, None), P("pu", "pv"))
    return jax.shard_map(
        per_device, mesh=mesh, in_specs=in_specs, out_specs=out_specs, check_vma=False
    )
```

time: 139 us -> 116 us (0.83)
  Pallas kernels: 131 us -> 114 us
  local copies, waits for them, and re-layouts: 6.42 us -> 0.69 us
    pallas_call x1, Pallas kernels: 127 us -> 109 us  [solve(): pl.pallas_call(solver_kernel, out_shape=(jax.ShapeDtypeStruct((6, 6, 128,...]
    unnamed x5 -> x3, local copies, waits for them, and re-layouts: 3.69 us -> 0.69 us
    reshape x2 -> x0, local copies, waits for them, and re-layouts: 2.73 us -> none  [the longest x1 1.4 us: solve(): links.reshape(6, 36)]
    pallas_call x1, Pallas kernels: 4.46 us -> 5.89 us  [copied(): pl.pallas_call(copy_kernel, out_shape=jax.ShapeDtypeStruct(value.shape, v...]
where the time goes in v3:
time: 116 us
  Pallas kernels  114 us (98%)
    pallas_call x1, Pallas kernels, solve(): pl.pallas_call(solver_kernel, out_shape=(jax.ShapeDtypeStruct((6, 6, 128,...  109 us
    pallas_call x1, Pallas kernels, copied(): pl.pallas_call(copy_kernel, out_shape=jax.ShapeDtypeStruct(value.shape, v...  5.89 us

profile of v3, /device:TPU:1, one launch (start us, length us, event | category | flops | bytes accessed | tf_op | source)
XLA Modules:
  0.0 115.8 jit_solution(14914115753572877196)
XLA Ops:
  0.6 108.6 %solver.1 = (bf16[6,6,128,768]{3,2,1,0:T(8,128)(2,1)}, f32[128,48]{1,0:T(8,128)}) custom-call(s32[6,6,6]{2,1,0:T(8,128)} %links.1, bf16[6,6,128,768]{3,2,1,0:T(8,128)(2,1)} %density.1, bf16[6,6,6,128,128]{4,3,2,1,0:T(8,128)(2,1)} %near_hbm.1, bf16[6,6,128,128]{3,2,1,0:T(8,128)(2,1)} %right_hbm.1, f32[4,2,128,128]{3,2,1,0:T(8,128)} %bitcast.2, ...), custom_call_target="tpu_custom_call" | custom-call | flops 10000000000 | bytes 33554432 | tf_op jit(solution)/shard_map/solver/pallas_call | solution.py:517
  109.2 0.0 copy-start
  109.2 5.9 %copy_out.1 = bf16[6,6,128,768]{3,2,1,0:T(8,128)(2,1)} custom-call(bf16[6,6,128,768]{3,2,1,0:T(8,128)(2,1)} %get-tuple-element.4.source), custom_call_target="tpu_custom_call" | custom-call | tf_op jit(solution)/shard_map/copy_out/pallas_call | solution.py:574
  115.1 0.0 copy-done
  115.1 0.7 copy.9
Async XLA Ops:
  109.2 5.9 %copy-start = (f32[128,48]{1,0:T(8,128)S(1)}, f32[128,48]{1,0:T(8,128)}, u32[]{:S(2)}) copy-start(f32[128,48]{1,0:T(8,128)} %get-tuple-element.7) | copy-start | bytes 73732

commit v4 on v3

--- a/solution.py
+++ b/solution.py
@@ -416,6 +416,12 @@
             def _(step=step):
                 w_copy(step, partners[step + 1]).start()
 
+        @pl.when(t > 0)
+        def _():
+            path[...] = dot_tn(halves[t], path[...]) + dot_tn(mixed[...], dot_tn(linv[t - 1], path[...]))
+
+        path[...] = dot_nn(linv[t], path[...])
+
         @pl.when(t < LEVELS - 1)
         def _():
             y_copy(t, 0, (u_core, v)).wait()
@@ -424,12 +430,6 @@
             part = part + dot_tn(mine[t + 1, 2:4].reshape(256, 128), other[t + 1, 2:4].reshape(256, 128))
             cross_send[t] = part
             cross_copy(t).start()
-
-        @pl.when(t > 0)
-        def _():
-            path[...] = dot_tn(halves[t], path[...]) + dot_tn(mixed[...], dot_tn(linv[t - 1], path[...]))
-
-        path[...] = dot_nn(linv[t], path[...])
 
         @pl.when((t == 4) & (core != x0))
         def _():

time: 116 us -> 114 us (0.983)
    pallas_call x1, Pallas kernels: 109 us -> 107 us  [solve(): pl.pallas_call(solver_kernel, out_shape=(jax.ShapeDtypeStruct((6, 6, 128,...]
where the time goes in v4:
time: 114 us
  Pallas kernels  113 us (99%)
    pallas_call x1, Pallas kernels, solve(): pl.pallas_call(solver_kernel, out_shape=(jax.ShapeDtypeStruct((6, 6, 128,...  107 us
    pallas_call x1, Pallas kernels, copied(): pl.pallas_call(copy_kernel, out_shape=jax.ShapeDtypeStruct(value.shape, v...  5.89 us

profile of v4, /device:TPU:1, one launch (start us, length us, event | category | flops | bytes accessed | tf_op | source)
XLA Modules:
  0.0 114.2 jit_solution(16532932338390379150)
XLA Ops:
  0.6 106.9 %solver.1 = (bf16[6,6,128,768]{3,2,1,0:T(8,128)(2,1)}, f32[128,48]{1,0:T(8,128)}) custom-call(s32[6,6,6]{2,1,0:T(8,128)} %links.1, bf16[6,6,128,768]{3,2,1,0:T(8,128)(2,1)} %density.1, bf16[6,6,6,128,128]{4,3,2,1,0:T(8,128)(2,1)} %near_hbm.1, bf16[6,6,128,128]{3,2,1,0:T(8,128)(2,1)} %right_hbm.1, f32[4,2,128,128]{3,2,1,0:T(8,128)} %bitcast.2, ...), custom_call_target="tpu_custom_call" | custom-call | flops 10000000000 | bytes 33554432 | tf_op jit(solution)/shard_map/solver/pallas_call | solution.py:517
  107.6 0.0 copy-start
  107.6 5.9 %copy_out.1 = bf16[6,6,128,768]{3,2,1,0:T(8,128)(2,1)} custom-call(bf16[6,6,128,768]{3,2,1,0:T(8,128)(2,1)} %get-tuple-element.4.source), custom_call_target="tpu_custom_call" | custom-call | tf_op jit(solution)/shard_map/copy_out/pallas_call | solution.py:574
  113.5 0.0 copy-done
  113.5 0.7 copy.9
Async XLA Ops:
  107.6 5.9 %copy-start = (f32[128,48]{1,0:T(8,128)S(1)}, f32[128,48]{1,0:T(8,128)}, u32[]{:S(2)}) copy-start(f32[128,48]{1,0:T(8,128)} %get-tuple-element.7) | copy-start | bytes 73732

commit v5 on v4

--- a/solution.py
+++ b/solution.py
@@ -396,8 +396,7 @@
             leaf_gram_copy(1).start()
             leaf_gram_copy(0).wait()
             gram[...] = part + cross_recv[LEVELS]
-            leaf_gram_copy(1).wait()
-            path[...] = jnp.where(core == 0, ours, theirs) + cross_recv[LEVELS + 1]
+            mixed[...] = jnp.where(core == 0, ours, theirs)
 
         @pl.when(t > 0)
         def _():
@@ -415,6 +414,11 @@
             @pl.when(t == step)
             def _(step=step):
                 w_copy(step, partners[step + 1]).start()
+
+        @pl.when(t == 0)
+        def _():
+            leaf_gram_copy(1).wait()
+            path[...] = mixed[...] + cross_recv[LEVELS + 1]
 
         @pl.when(t > 0)
         def _():

time: 114 us -> 114 us (level)
  no operation moved by 1% of the time
where the time goes in v5:
time: 114 us
  Pallas kernels  113 us (99%)
    pallas_call x1, Pallas kernels, solve(): pl.pallas_call(solver_kernel, out_shape=(jax.ShapeDtypeStruct((6, 6, 128,...  107 us
    pallas_call x1, Pallas kernels, copied(): pl.pallas_call(copy_kernel, out_shape=jax.ShapeDtypeStruct(value.shape, v...  5.89 us

profile of v5, /device:TPU:1, one launch (start us, length us, event | category | flops | bytes accessed | tf_op | source)
XLA Modules:
  0.0 114.2 jit_solution(17447601846200740382)
XLA Ops:
  0.6 106.9 %solver.1 = (bf16[6,6,128,768]{3,2,1,0:T(8,128)(2,1)}, f32[128,48]{1,0:T(8,128)}) custom-call(s32[6,6,6]{2,1,0:T(8,128)} %links.1, bf16[6,6,128,768]{3,2,1,0:T(8,128)(2,1)} %density.1, bf16[6,6,6,128,128]{4,3,2,1,0:T(8,128)(2,1)} %near_hbm.1, bf16[6,6,128,128]{3,2,1,0:T(8,128)(2,1)} %right_hbm.1, f32[4,2,128,128]{3,2,1,0:T(8,128)} %bitcast.2, ...), custom_call_target="tpu_custom_call" | custom-call | flops 10000000000 | bytes 33554432 | tf_op jit(solution)/shard_map/solver/pallas_call | solution.py:521
  107.6 0.0 copy-start
  107.6 5.9 %copy_out.1 = bf16[6,6,128,768]{3,2,1,0:T(8,128)(2,1)} custom-call(bf16[6,6,128,768]{3,2,1,0:T(8,128)(2,1)} %get-tuple-element.4.source), custom_call_target="tpu_custom_call" | custom-call | tf_op jit(solution)/shard_map/copy_out/pallas_call | solution.py:578
  113.5 0.0 copy-done
  113.5 0.7 copy.9
Async XLA Ops:
  107.6 5.9 %copy-start = (f32[128,48]{1,0:T(8,128)S(1)}, f32[128,48]{1,0:T(8,128)}, u32[]{:S(2)}) copy-start(f32[128,48]{1,0:T(8,128)} %get-tuple-element.7) | copy-start | bytes 73732
